TPU v7x, 32 devices: a whole 2x2x4 slice. The times are simulated.
32 devices in a mesh: fsdp: 32 (over z, y, x, core).
Axes of the slice: x: 2, y: 2, z: 4, core: 2. Of those that a mesh axis runs over, the one named last changes fastest.
Arguments:
- src_in: bfloat16 [32768, 512], P('fsdp'), may hold values from -6 to 6
- tgt_in: bfloat16 [32768, 512], P('fsdp'), may hold values from -6 to 6
- src_len: int32 [32, 16], P('fsdp'), may hold values from 0 to 250, as said below
- tgt_len: int32 [32, 16], P('fsdp'), may hold values from 0 to 250, as said below
- tgt_mask: int32 [32768], P('fsdp'), may hold values 0 or 1
- enc_cot: bfloat16 [32768, 512], P('fsdp'), may hold values from -6 to 6
- dec_cot: bfloat16 [32768, 512], P('fsdp'), may hold values from -6 to 6
- enc_master: float32 [6144, 512], P('fsdp')
- enc_first: float32 [6144, 512], P('fsdp')
- enc_second: float32 [6144, 512], P('fsdp'), as said below
- dec_master: float32 [8192, 512], P('fsdp')
- dec_first: float32 [8192, 512], P('fsdp')
- dec_second: float32 [8192, 512], P('fsdp'), as said below
- small_master: float32 [11, 512], P(None, 'fsdp')
- small_first: float32 [11, 512], P(None, 'fsdp')
- small_second: float32 [11, 512], P(None, 'fsdp'), as said below
Outputs:
- enc_out: bfloat16 [32768, 512], P('fsdp')
- dec_out: bfloat16 [32768, 512], P('fsdp')
- src_grad: float32 [32768, 512], P('fsdp')
- tgt_grad: float32 [32768, 512], P('fsdp')
- enc_new: float32 [6144, 512], P('fsdp')
- enc_first_new: float32 [6144, 512], P('fsdp')
- encoder_second_moment_updated: float32 [6144, 512], P('fsdp')
- enc_copy_new: bfloat16 [6144, 512], P('fsdp')
- dec_new: float32 [8192, 512], P('fsdp')
- dec_first_new: float32 [8192, 512], P('fsdp')
- dec_second_new: float32 [8192, 512], P('fsdp')
- dec_copy_new: bfloat16 [8192, 512], P('fsdp')
- small_grad: float32 [11, 512], P(None, 'fsdp')
- small_first_new: float32 [11, 512], P(None, 'fsdp')
- small_second_new: float32 [11, 512], P(None, 'fsdp')
Inputs may be any that keep to these rules, and one draw needn't show every extreme that they name: `src_len`: nonzero lengths are at least 5; zeros stand only after all nonzero entries of a row; a row sums to at most 1024; every row holds the length 250. `tgt_len`: zero exactly where src_len is zero; nonzero lengths are at least 5; a row sums to at most 1024; every row holds the length 250. `enc_second`: Positive. `dec_second`: Positive. `small_second`: Positive.
All inputs are finite; a program needn't handle non-finite values. No bound on the sum of `tgt_mask` on one device may be relied on, other than what follows from the above.
Results may differ from a plain program's by a relative error of at most 0.02.
The roundings to bfloat16 on the way count: a program that leaves them out, or rounds other values in their place, can miss the bound.
Values may be sent and summed in bfloat16 or wider, within the bound.
No kernel may reach another device: no remote copies, remote signals or barrier semaphores. Data moves between devices by JAX's collectives and lax.ppermute only.
A program may use at most 256 MiB of HBM per device.

v0:
```python
import functools

import jax
import jax.numpy as jnp
from jax import lax
from jax.experimental import pallas as pl
from jax.experimental.pallas import tpu as pltpu
from jax.sharding import PartitionSpec as P

HEADS = 8
HEAD = 64
STEPS = 7
TILE = 256
LANES = 128

rate = 0.02
beta_one = 0.9
beta_two = 0.98
epsilon = 1e-06
decay = 0.01
floor_value = -1000000000.0
root_half = 0.7071067811865476
inverse_root_tau = 0.3989422804014327

F32 = jnp.float32
LOW = jnp.bfloat16
MIB = 2**20


def nn(former, latter):
    return lax.dot_general(
        former, latter, (((1,), (0,)), ((), ())), preferred_element_type=F32
    )


def nt(former, latter):
    return lax.dot_general(
        former, latter, (((1,), (1,)), ((), ())), preferred_element_type=F32
    )


def turned(values):
    return values.astype(F32).T.astype(LOW)


def column_of(row):
    return jnp.broadcast_to(row, (8, row.shape[1])).T[:, 0:1]


def ln_forward(values, gain, shift):
    centered = values - jnp.mean(values, axis=-1, keepdims=True)
    spread = jnp.mean(centered * centered, axis=-1, keepdims=True)
    inverse = lax.rsqrt(spread + 1e-05)
    normed = centered * inverse
    return normed * gain + shift, normed, inverse


def ln_backward(upstream, normed, inverse, gain):
    scaled = upstream * gain
    first = jnp.mean(scaled, axis=-1, keepdims=True)
    second = jnp.mean(scaled * normed, axis=-1, keepdims=True)
    return inverse * (scaled - first - normed * second)


def phi_and_slope(values):
    phi = 0.5 + 0.5 * lax.erf(values * root_half)
    return phi, phi + values * (jnp.exp(-0.5 * (values * values)) * inverse_root_tau)


def one_head(pair, head):
    lane = lax.broadcasted_iota(jnp.int32, pair.shape, 1)
    keep = lane < HEAD if head % 2 == 0 else lane >= HEAD
    return jnp.where(keep, pair, jnp.zeros_like(pair))


def pair_columns(head):
    return slice(LANES * (head // 2), LANES * (head // 2) + LANES)


def head_rows(head):
    return slice(HEAD * head, HEAD * head + HEAD)


def block_of(ref, j, count):
    if count == 1:
        return ref[...]
    return jnp.concatenate(
        [ref[first + 16 * j : first + 16 * j + 16, :] for first in range(0, ref.shape[0], 16 * count)], axis=0
    )


def spread(wide, values):
    for n in range(wide.shape[0]):
        wide[n] = values[:, LANES * n : LANES * n + LANES].astype(F32)


def third_rows(wide, j):
    rows = pl.ds(j, wide.shape[1] // 3, stride=3)
    return jnp.concatenate([wide[n, rows, :] for n in range(wide.shape[0])], axis=1).astype(LOW)


def put_third_rows(wide, j, values):
    rows = pl.ds(j, wide.shape[1] // 3, stride=3)
    for n in range(wide.shape[0]):
        wide[n, rows, :] = values[:, LANES * n : LANES * n + LANES]


def wide_scratch(width):
    return pltpu.VMEM((width // LANES, 3 * width, LANES), F32)


def put_block(ref, j, values):
    ref[:, j] = values.reshape(ref.shape[0], ref.shape[2], ref.shape[3])


OWNERS = 32


def row_copies(first, last, own, paired):
    found = []
    at = first
    while at < last:
        owner = at // own
        end = min(last, (owner + 1) * own)
        half = OWNERS // 4
        place = (2 * (owner // 2 // half) + owner % 2, owner // 2 % half) if paired else (0, owner)
        found.append((*place, at - owner * own, end - at, at - first))
        at = end
    return found


class Fetch:
    def __init__(self, far, core, copies, near, semaphores, used):
        self.core = core

        def handles(side):
            return [
                pltpu.make_async_copy(
                    far[source ^ side].at[owner, pl.ds(row, rows)], near.at[pl.ds(to, rows)], semaphores.at[used + n]
                )
                for n, (source, owner, row, rows, to) in enumerate(copies)
            ]

        self.handles = handles

    def start(self):
        if self.core is None:
            for handle in self.handles(0):
                handle.start()
            return
        for side in (0, 1):

            @pl.when(self.core == side)
            def _(side=side):
                for handle in self.handles(side):
                    handle.start()

    def wait(self):
        for handle in self.handles(0):
            handle.wait()


def fetches(far, plan, wanted, nears, semaphores):
    used = 0
    made = []
    core = plan[2, 1] if len(far) > 1 else None
    for copies, near in zip(wanted, nears):
        made.append(Fetch(far, core, copies, near, semaphores, used))
        used += len(copies)
    return made


def wait_first(i, loads):
    @pl.when(i == 0)
    def _():
        for load in loads:
            load.wait()


def fetch_scratch(wanted, width):
    return [pltpu.VMEM((sum(c[3] for c in copies), width), LOW) for copies in wanted] + [
        pltpu.SemaphoreType.DMA((sum(len(copies) for copies in wanted),))
    ]


FAR = pl.BlockSpec(memory_space=pl.ANY)


def sources_of(wanted):
    last = max(copy[0] for copies in wanted for copy in copies)
    return 1 if last == 0 else 2 * (last // 2) + 2


def call(kernel, grid, in_specs, out_specs, out_shape, scratch, flops, moved, name, room=24, near=(), keep=()):
    single = not isinstance(out_shape, list)
    shapes = [
        (pltpu.VMEM if keep is True or n in keep else pltpu.HBM)(*made)
        for n, made in enumerate([out_shape] if single else out_shape)
    ]
    made = pl.pallas_call(
        kernel,
        grid_spec=pltpu.PrefetchScalarGridSpec(
            num_scalar_prefetch=1,
            grid=grid,
            in_specs=in_specs,
            out_specs=out_specs,
            scratch_shapes=scratch,
        ),
        out_shape=shapes[0] if single else shapes,
        compiler_params=pltpu.CompilerParams(vmem_limit_bytes=room * MIB),
        cost_estimate=pl.CostEstimate(
            flops=flops, bytes_accessed=moved, transcendentals=0
        ),
        name=name,
    )

    def run(plan, *operands):
        placed = [
            operand
            if near is True or n in near
            else pltpu.with_memory_space_constraint(operand, pltpu.HBM)
            for n, operand in enumerate(operands)
        ]
        return made(plan, *placed)

    return run


def whole(shape):
    zeros = (0,) * len(shape)
    return pl.BlockSpec(shape, lambda i, *_: zeros)


def rows_of(width):
    return pl.BlockSpec((TILE, width), lambda i, *_: (i, 0))


def at_block(shape, *index):
    return pl.BlockSpec(shape, lambda i, *_: index)


def shaped(shape, kind):
    return (shape, kind)


def attend_tile(plan, i, keys, key_cols, query, owner_row, key_owner, vt, sc):
    scores, acc, top, total, masked_q = sc
    query = query * jnp.asarray(HEAD**-0.5, LOW)
    for h in range(HEADS):
        masked_q[h] = one_head(query[:, pair_columns(h)], h)
    top[...] = jnp.full_like(top, -1e30)
    total[...] = jnp.zeros_like(total)
    acc[...] = jnp.zeros_like(acc)
    begin = plan[0, i]
    chunks = plan[1, i]

    def score_tile(j, carry):
        rows = pl.ds(pl.multiple_of(begin + j * TILE, LANES), TILE)
        bias = jnp.where(key_owner[rows, 0:1] == owner_row, 0.0, floor_value)
        tops = []
        for h in range(HEADS):
            cols = pl.ds(key_cols + LANES * (h // 2), LANES)
            s = nt(keys[rows, cols], masked_q[h]) + bias
            scores[j, h] = s
            tops.append(jnp.max(s, axis=0, keepdims=True))
        top[...] = jnp.maximum(top[...], jnp.concatenate(tops, axis=0))
        return carry

    lax.fori_loop(0, chunks, score_tile, 0)

    def weigh_tile(j, carry):
        rows = pl.ds(pl.multiple_of(begin + j * TILE, LANES), TILE)
        sums = []
        for h in range(HEADS):
            p = jnp.exp(scores[j, h] - top[h : h + 1, :])
            sums.append(jnp.sum(p, axis=0, keepdims=True))
            acc[head_rows(h), :] += nn(vt[head_rows(h), rows], p.astype(LOW))
        total[...] += jnp.concatenate(sums, axis=0)
        return carry

    lax.fori_loop(0, chunks, weigh_tile, 0)


def fwd_block_kernel(plan, *refs, cross, gain_row, wanted, packed, ffn):
    refs = list(refs)

    def next_refs(count):
        taken = refs[:count]
        del refs[:count]
        return taken

    if cross:
        normed_in, memory = next_refs(2)
    else:
        (x_all,) = next_refs(1)
    far = next_refs(sources_of(wanted))
    small, owner_q, owner_k = next_refs(3)
    q_out, kv_out, ctx_out, lse_out, normed_out, inverse_out = next_refs(6)
    if ffn:
        out, normed_last, inverse_last = next_refs(3)
    kv, vt, mean_v, key_owner, scores, acc, top, total, masked_q, q_all = next_refs(10)
    nears = next_refs(len(wanted))
    semaphores = refs.pop(0)
    loads = fetches(far, plan, wanted, nears, semaphores)
    i = pl.program_id(0)
    width = kv.shape[1] // 2

    @pl.when(i == 0)
    def _():
        for load in loads:
            load.start()
        key_owner[...] = jnp.broadcast_to(owner_k[...], (8, owner_k.shape[1])).T
        loads[0].wait()
        if cross:
            wk, wv = block_of(nears[0], 0, 2), block_of(nears[0], 1, 2)
        elif packed:
            wq, wk, wv = (block_of(nears[0], j, 3) for j in range(3))
        else:
            wide = refs[0]
            spread(wide, nears[0][...])
            wq, wk, wv = (third_rows(wide, j) for j in range(3))
        sums = jnp.zeros((1, width), F32)
        for t in range(kv.shape[0] // TILE):
            rows = slice(t * TILE, t * TILE + TILE)
            x = memory[rows, :] if cross else x_all[rows, :]
            if not cross:
                q_all[rows, :] = nn(x, wq).astype(LOW)
            kv[rows, :width] = nn(x, wk).astype(LOW)
            v = nn(x, wv).astype(LOW)
            kv[rows, width:] = v
            v = v.astype(F32)
            vt[:, rows] = v.T.astype(LOW)
            sums = sums + jnp.sum(v, axis=0, keepdims=True)
        mean_v[...] = sums * (1.0 / kv.shape[0])
        for load in loads[1 : 3 if cross else 2]:
            load.wait()

    wo = nears[1]
    mine = pl.ds(pl.multiple_of(i * TILE, TILE), TILE)
    if cross:
        resid = normed_in[...] * small[4:5, :] + small[5:6, :]
        query = nn(resid.astype(LOW), nears[2][...]).astype(LOW)
        q_out[...] = query
    else:
        resid = x_all[mine, :].astype(F32)
        query = q_all[mine, :]
        q_out[...] = query
    kv_out[...] = kv[mine, :]
    owner_row = owner_q[...]
    attend_tile(plan, i, kv, 0, query, owner_row, key_owner, vt, (scores, acc, top, total, masked_q))
    dead = owner_row < 0
    sums = jnp.where(dead, 1.0, total[...])
    share = 1.0 / sums
    lse_out[...] = jnp.where(dead, 0.0, top[...] + jnp.log(sums))
    for h in range(HEADS):
        acc[head_rows(h), :] = acc[head_rows(h), :] * share[h : h + 1, :]
    live = column_of(owner_row) >= 0
    context = jnp.where(live, acc[...].T, mean_v[...]).astype(LOW)
    ctx_out[...] = context
    added = nn(context, wo[...]) * live.astype(F32)
    mid, normed, inverse = ln_forward(
        resid + added, small[gain_row : gain_row + 1, :], small[gain_row + 1 : gain_row + 2, :]
    )
    normed_out[...] = normed
    inverse_out[...] = jnp.broadcast_to(inverse, inverse_out.shape)
    if ffn:
        wup, wdown = nears[-2:]
        wait_first(i, loads[-2:])
        blocks = wdown.shape[0] // width
        low = mid.astype(LOW)
        result = mid
        for j in range(blocks):
            inner = nn(low, block_of(wup, j, blocks))
            phi = 0.5 + 0.5 * lax.erf(inner * root_half)
            result = result + nn((inner * phi).astype(LOW), wdown[j * width : j * width + width, :])
        result, normed, inverse = ln_forward(
            result, small[gain_row + 2 : gain_row + 3, :], small[gain_row + 3 : gain_row + 4, :]
        )
        out[...] = result.astype(LOW)
        normed_last[...] = normed
        inverse_last[...] = jnp.broadcast_to(inverse, inverse_last.shape)


def attention_scratch(keys, width):
    return [
        pltpu.VMEM((keys, 2 * width), LOW),
        pltpu.VMEM((width, keys), LOW),
        pltpu.VMEM((1, width), F32),
        pltpu.VMEM((keys, 8), F32),
        pltpu.VMEM((keys // TILE, HEADS, TILE, TILE), F32),
        pltpu.VMEM((width, TILE), F32),
        pltpu.VMEM((HEADS, TILE), F32),
        pltpu.VMEM((HEADS, TILE), F32),
        pltpu.VMEM((HEADS, TILE, LANES), LOW),
        pltpu.VMEM((keys, width), LOW),
    ]


def block_outs(queries, width):
    specs = [
        rows_of(width),
        rows_of(2 * width),
        rows_of(width),
        pl.BlockSpec((HEADS, TILE), lambda i, *_: (0, i)),
        rows_of(width),
        rows_of(LANES),
    ]
    shapes = [
        shaped((queries, width), LOW),
        shaped((queries, 2 * width), LOW),
        shaped((queries, width), LOW),
        shaped((HEADS, queries), F32),
        shaped((queries, width), F32),
        shaped((queries, LANES), F32),
    ]
    return specs, shapes


def owner_specs(keys):
    return [pl.BlockSpec((1, TILE), lambda i, *_: (0, i)), whole((1, keys))]


def fwd_block(plan, x, memory, far, wanted, packed, small, gain_row, owner, key_owner, ffn, name):
    cross = memory is not None
    number, width = x.shape
    specs, shapes = block_outs(number, width)
    if ffn:
        specs += [rows_of(width), rows_of(width), rows_of(LANES)]
        shapes += [shaped((number, width), LOW), shaped((number, width), F32), shaped((number, LANES), F32)]
    scratch = attention_scratch(number, width) + fetch_scratch(wanted, width)
    if not cross and not packed:
        scratch.append(wide_scratch(width))
    return call(
        functools.partial(
            fwd_block_kernel, cross=cross, gain_row=gain_row, wanted=wanted, packed=packed, ffn=ffn
        ),
        (number // TILE,),
        ([rows_of(width), whole(memory.shape)] if cross else [whole(x.shape)])
        + [FAR] * sources_of(wanted)
        + [whole(small.shape)]
        + owner_specs(number),
        specs,
        shapes,
        scratch,
        8 * number * width * width + number * number * width * 2,
        16 * number * width,
        name,
        room=44,
    )(plan, *([x, memory] if cross else [x]), *far[: sources_of(wanted)], small, owner, key_owner)


def ffn_back_kernel(plan, *refs, tiles, summed, gain_row, wanted):
    refs = list(refs)
    cot = refs.pop(0)
    extra = refs.pop(0) if summed else None
    normed_top, inverse_top, normed_mid, inverse_mid, context = refs[:5]
    far = refs[5 : 5 + sources_of(wanted)]
    (small,
     d_sum, d_context, g_up, g_down, g_out, sums, hidden, d_inner, mid_low, d_down, d_product,
     wup, wdown, wo, semaphores) = refs[5 + sources_of(wanted) :]
    loads = fetches(far, plan, wanted, (wup, wdown, wo), semaphores)
    i = pl.program_id(0)
    width = small.shape[1]
    blocks = wdown.shape[0] // width

    @pl.when(i == 0)
    def _():
        for load in loads:
            load.start()
        sums[...] = jnp.zeros_like(sums)

    @pl.when(i < tiles)
    def _():
        mine = pl.ds(pl.multiple_of(i * TILE, TILE), TILE)
        upstream = cot[...].astype(F32)
        if summed:
            upstream = upstream + extra[...]
        top = normed_top[...]
        sums[2:3, :] += jnp.sum(upstream * top, axis=0, keepdims=True)
        sums[3:4, :] += jnp.sum(upstream, axis=0, keepdims=True)
        d_mid = ln_backward(upstream, top, inverse_top[:, 0:1], small[gain_row + 2 : gain_row + 3, :])
        low = d_mid.astype(LOW)
        d_down[mine, :] = low
        normed = normed_mid[...]
        mid = (normed * small[gain_row : gain_row + 1, :] + small[gain_row + 1 : gain_row + 2, :]).astype(LOW)
        mid_low[mine, :] = mid
        wait_first(i, loads)
        for j in range(blocks):
            cols = slice(j * width, j * width + width)
            up = block_of(wup, j, blocks)
            inner = nn(mid, up)
            phi, slope = phi_and_slope(inner)
            hidden[j, mine, :] = (inner * phi).astype(LOW)
            part = (nt(low, wdown[cols, :]) * slope).astype(LOW)
            d_inner[j, mine, :] = part
            d_mid = d_mid + nt(part, up)
        sums[0:1, :] += jnp.sum(d_mid * normed, axis=0, keepdims=True)
        sums[1:2, :] += jnp.sum(d_mid, axis=0, keepdims=True)
        total = ln_backward(d_mid, normed, inverse_mid[:, 0:1], small[gain_row : gain_row + 1, :])
        d_sum[...] = total
        place = lax.broadcasted_iota(jnp.int32, (TILE, 1), 0) + i * TILE
        live = (place < plan[2, 0]).astype(F32)
        product = (total * live).astype(LOW)
        d_product[mine, :] = product
        d_context[...] = nt(product, wo[...]).astype(LOW)

    @pl.when(i >= tiles)
    def _():
        j = i - tiles
        put_block(g_up, 0, nn(turned(mid_low[...]), d_inner[j]).astype(LOW))
        g_down[...] = nn(turned(hidden[j]), d_down[...]).astype(LOW)

    @pl.when(i == tiles)
    def _():
        g_out[...] = nn(turned(context[...]), d_product[...]).astype(LOW)


def ffn_backward(plan, cots, top, mid, context, far, wanted, small, gain_row, inner, name):
    number, width = mid[0].shape
    tiles, blocks = number // TILE, inner // width

    def tile_of(columns):
        return pl.BlockSpec((TILE, columns), lambda i, *_: (jnp.minimum(i, tiles - 1), 0))

    return call(
        functools.partial(
            ffn_back_kernel, tiles=tiles, summed=len(cots) == 2, gain_row=gain_row, wanted=wanted
        ),
        (tiles + blocks,),
        [tile_of(width)] * len(cots)
        + [tile_of(width), tile_of(LANES), tile_of(width), tile_of(LANES), whole((number, width))]
        + [FAR] * sources_of(wanted)
        + [whole(small.shape)],
        [
            tile_of(width),
            tile_of(width),
            pl.BlockSpec((width // 16, 1, 16, width), lambda i, *_: (0, jnp.maximum(i - tiles, 0), 0, 0)),
            pl.BlockSpec((width, width), lambda i, *_: (jnp.maximum(i - tiles, 0), 0)),
            pl.BlockSpec((width, width), lambda i, *_: (0, 0)),
            pl.BlockSpec((8, width), lambda i, *_: (0, 0)),
        ],
        [
            shaped((number, width), F32),
            shaped((number, width), LOW),
            shaped((width // 16, blocks, 16, width), LOW),
            shaped((inner, width), LOW),
            shaped((width, width), LOW),
            shaped((8, width), F32),
        ],
        [
            pltpu.VMEM((blocks, number, width), LOW),
            pltpu.VMEM((blocks, number, width), LOW),
            pltpu.VMEM((number, width), LOW),
            pltpu.VMEM((number, width), LOW),
            pltpu.VMEM((number, width), LOW),
        ]
        + fetch_scratch(wanted, width),
        10 * number * width * inner,
        30 * number * width,
        name,
        room=44,
    )(plan, *cots, *top, *mid, context, *far[: sources_of(wanted)], small)


def turn_kernel(plan, *refs, tiles, gain_row, wanted):
    normed_in, memory, cot = refs[:3]
    far = refs[3 : 3 + sources_of(wanted)]
    (small, owner_q, owner_k,
     q_out, kv_out, lse_out, out, d_sum, d_context, g_up, g_down, g_out, sums,
     kv, vt, mean_v, key_owner, scores, acc, top, total, masked_q,
     hidden, d_inner, mid_low, d_down, d_product, contexts, slopes,
     *nears, semaphores) = refs[3 + sources_of(wanted) :]
    wkv, wo, wq, wup, wdown = nears
    loads = fetches(far, plan, wanted, nears, semaphores)
    i = pl.program_id(0)
    width = small.shape[1]
    blocks = wdown.shape[0] // width

    @pl.when(i == 0)
    def _():
        for load in loads:
            load.start()
        sums[...] = jnp.zeros_like(sums)
        key_owner[...] = jnp.broadcast_to(owner_k[...], (8, owner_k.shape[1])).T
        loads[0].wait()
        wk, wv = block_of(wkv, 0, 2), block_of(wkv, 1, 2)
        means = jnp.zeros((1, width), F32)
        for t in range(kv.shape[0] // TILE):
            rows = slice(t * TILE, t * TILE + TILE)
            x = memory[rows, :]
            kv[rows, :width] = nn(x, wk).astype(LOW)
            v = nn(x, wv).astype(LOW)
            kv[rows, width:] = v
            v = v.astype(F32)
            vt[:, rows] = v.T.astype(LOW)
            means = means + jnp.sum(v, axis=0, keepdims=True)
        mean_v[...] = means * (1.0 / kv.shape[0])
        for load in loads[1:3]:
            load.wait()

    @pl.when(i < tiles)
    def _():
        mine = pl.ds(pl.multiple_of(i * TILE, TILE), TILE)
        resid = normed_in[...] * small[gain_row - 2 : gain_row - 1, :] + small[gain_row - 1 : gain_row, :]
        query = nn(resid.astype(LOW), wq[...]).astype(LOW)
        q_out[...] = query
        kv_out[...] = kv[mine, :]
        owner_row = owner_q[...]
        attend_tile(
            plan, i, kv, 0, query, owner_row, key_owner, vt, (scores, acc, top, total, masked_q)
        )
        dead = owner_row < 0
        weighed = jnp.where(dead, 1.0, total[...])
        share = 1.0 / weighed
        lse_out[...] = jnp.where(dead, 0.0, top[...] + jnp.log(weighed))
        for h in range(HEADS):
            acc[head_rows(h), :] = acc[head_rows(h), :] * share[h : h + 1, :]
        live = column_of(owner_row) >= 0
        context = jnp.where(live, acc[...].T, mean_v[...]).astype(LOW)
        contexts[mine, :] = context
        added = nn(context, wo[...]) * live.astype(F32)
        mid, normed_mid, inverse_mid = ln_forward(
            resid + added, small[gain_row : gain_row + 1, :], small[gain_row + 1 : gain_row + 2, :]
        )
        wait_first(i, loads[3:])
        low = mid.astype(LOW)
        mid_low[mine, :] = low
        result = mid
        for j in range(blocks):
            inner = nn(low, block_of(wup, j, blocks))
            phi, slope = phi_and_slope(inner)
            made = (inner * phi).astype(LOW)
            hidden[j, mine, :] = made
            slopes[j] = slope
            result = result + nn(made, wdown[j * width : j * width + width, :])
        result, normed, inverse = ln_forward(
            result, small[gain_row + 2 : gain_row + 3, :], small[gain_row + 3 : gain_row + 4, :]
        )
        out[...] = result.astype(LOW)

        upstream = cot[...].astype(F32)
        sums[2:3, :] += jnp.sum(upstream * normed, axis=0, keepdims=True)
        sums[3:4, :] += jnp.sum(upstream, axis=0, keepdims=True)
        d_mid = ln_backward(upstream, normed, inverse, small[gain_row + 2 : gain_row + 3, :])
        low = d_mid.astype(LOW)
        d_down[mine, :] = low
        for j in range(blocks):
            part = (nt(low, wdown[j * width : j * width + width, :]) * slopes[j]).astype(LOW)
            d_inner[j, mine, :] = part
            d_mid = d_mid + nt(part, block_of(wup, j, blocks))
        sums[0:1, :] += jnp.sum(d_mid * normed_mid, axis=0, keepdims=True)
        sums[1:2, :] += jnp.sum(d_mid, axis=0, keepdims=True)
        d_all = ln_backward(d_mid, normed_mid, inverse_mid, small[gain_row : gain_row + 1, :])
        d_sum[...] = d_all
        product = (d_all * live.astype(F32)).astype(LOW)
        d_product[mine, :] = product
        d_context[...] = nt(product, wo[...]).astype(LOW)

    @pl.when(i >= tiles)
    def _():
        j = i - tiles
        put_block(g_up, 0, nn(turned(mid_low[...]), d_inner[j]).astype(LOW))
        g_down[...] = nn(turned(hidden[j]), d_down[...]).astype(LOW)

    @pl.when(i == tiles)
    def _():
        g_out[...] = nn(turned(contexts[...]), d_product[...]).astype(LOW)


def cross_turn(plan, normed, memory, cot, far, wanted, small, gain_row, owner, key_owner, inner, name):
    number, width = normed.shape
    keys = memory.shape[0]
    tiles, blocks = number // TILE, inner // width

    def tile_of(columns):
        return pl.BlockSpec((TILE, columns), lambda i, *_: (jnp.minimum(i, tiles - 1), 0))

    def columns_of(rows):
        return pl.BlockSpec((rows, TILE), lambda i, *_: (0, jnp.minimum(i, tiles - 1)))

    return call(
        functools.partial(turn_kernel, tiles=tiles, gain_row=gain_row, wanted=wanted),
        (tiles + blocks,),
        [tile_of(width), whole(memory.shape), tile_of(width)]
        + [FAR] * sources_of(wanted)
        + [whole(small.shape), columns_of(1), whole((1, keys))],
        [
            tile_of(width),
            tile_of(2 * width),
            columns_of(HEADS),
            tile_of(width),
            tile_of(width),
            tile_of(width),
            pl.BlockSpec((width // 16, 1, 16, width), lambda i, *_: (0, jnp.maximum(i - tiles, 0), 0, 0)),
            pl.BlockSpec((width, width), lambda i, *_: (jnp.maximum(i - tiles, 0), 0)),
            whole((width, width)),
            whole((8, width)),
        ],
        [
            shaped((number, width), LOW),
            shaped((number, 2 * width), LOW),
            shaped((HEADS, number), F32),
            shaped((number, width), LOW),
            shaped((number, width), F32),
            shaped((number, width), LOW),
            shaped((width // 16, blocks, 16, width), LOW),
            shaped((inner, width), LOW),
            shaped((width, width), LOW),
            shaped((8, width), F32),
        ],
        attention_scratch(keys, width)[:-1]
        + [
            pltpu.VMEM((blocks, number, width), LOW),
            pltpu.VMEM((blocks, number, width), LOW),
            pltpu.VMEM((number, width), LOW),
            pltpu.VMEM((number, width), LOW),
            pltpu.VMEM((number, width), LOW),
            pltpu.VMEM((number, width), LOW),
            pltpu.VMEM((blocks, TILE, width), F32),
        ]
        + fetch_scratch(wanted, width),
        12 * number * width * inner + number * number * width * 2,
        30 * number * width,
        name,
        room=58,
    )(plan, normed, memory, cot, *far[: sources_of(wanted)], small, owner, key_owner)


def attend_back(plan, i, q_ref, k_ref, v_ref, do_ref, lse, owner_q, owner_k, scratch):
    kt, key_owner, masked_q, masked_do, dqt, dk_sum, dv_sum, weights, d_weights, dots = scratch

    @pl.when(i == 0)
    def _():
        key_owner[...] = jnp.broadcast_to(owner_k[...], (8, owner_k.shape[1])).T
        kt[...] = turned(k_ref[...])
        dk_sum[...] = jnp.zeros_like(dk_sum)
        dv_sum[...] = jnp.zeros_like(dv_sum)

    query = q_ref[...] * jnp.asarray(HEAD**-0.5, LOW)
    upstream = do_ref[...]
    for h in range(HEADS):
        masked_q[h] = one_head(query[:, pair_columns(h)], h)
        masked_do[h] = one_head(upstream[:, pair_columns(h)], h)
    dqt[...] = jnp.zeros_like(dqt)
    dots[...] = jnp.zeros_like(dots)
    owner_row = owner_q[...]
    begin = plan[0, i]
    chunks = plan[1, i]

    def weigh_tile(j, carry):
        rows = pl.ds(pl.multiple_of(begin + j * TILE, LANES), TILE)
        bias = jnp.where(key_owner[rows, 0:1] == owner_row, 0.0, floor_value)
        sums = []
        for h in range(HEADS):
            s = nt(k_ref[rows, pair_columns(h)], masked_q[h])
            p = jnp.exp((s - lse[h : h + 1, :]) + bias)
            dp = nt(v_ref[rows, pair_columns(h)], masked_do[h])
            weights[j, h] = p
            d_weights[j, h] = dp
            sums.append(jnp.sum(p * dp, axis=0, keepdims=True))
        dots[...] += jnp.concatenate(sums, axis=0)
        return carry

    lax.fori_loop(0, chunks, weigh_tile, 0)

    def grad_tile(j, carry):
        rows = pl.ds(pl.multiple_of(begin + j * TILE, LANES), TILE)
        for pair in range(HEADS // 2):
            cols = pair_columns(2 * pair)
            dv_part = dv_sum[rows, cols]
            dk_part = dk_sum[rows, cols]
            for h in (2 * pair, 2 * pair + 1):
                p = weights[j, h]
                ds = (p * (d_weights[j, h] - dots[h : h + 1, :])).astype(LOW)
                dv_part = dv_part + nn(p.astype(LOW), masked_do[h])
                dk_part = dk_part + nn(ds, masked_q[h])
                dqt[head_rows(h), :] += nn(kt[head_rows(h), rows], ds)
            dv_sum[rows, cols] = dv_part
            dk_sum[rows, cols] = dk_part
        return carry

    lax.fori_loop(0, chunks, grad_tile, 0)
    return (dqt[...] * HEAD**-0.5).T.astype(LOW)


def attention_back_kernel(plan, *refs, made):
    q_ref, k_ref, v_ref, do_ref, lse, owner_q, owner_k, *refs = refs
    x = refs.pop(0) if made else None
    dq, dk, dv, *refs = refs
    g_qkv = refs.pop(0) if made else None
    scratch, more = refs[:10], refs[10:]
    dk_sum, dv_sum = scratch[5:7]
    i = pl.program_id(0)
    dq_tile = attend_back(plan, i, q_ref, k_ref, v_ref, do_ref, lse, owner_q, owner_k, scratch)
    dq[...] = dq_tile
    if made:
        dq_all = more[0]
        dq_all[pl.ds(pl.multiple_of(i * TILE, TILE), TILE), :] = dq_tile

    @pl.when(i == pl.num_programs(0) - 1)
    def _():
        dk[...] = dk_sum[...].astype(LOW)
        dv[...] = dv_sum[...].astype(LOW)
        if made:
            turn = turned(x[...])
            for j, ref in enumerate((dq_all, dk, dv)):
                grad = nn(turn, ref[...])
                if made == "units":
                    put_block(g_qkv, j, grad.astype(LOW))
                else:
                    put_third_rows(more[1], j, grad)
        if made == "rows":
            for n in range(more[1].shape[0]):
                g_qkv[:, LANES * n : LANES * n + LANES] = more[1][n].astype(LOW)


def attend_back_scratch(keys, width):
    return [
        pltpu.VMEM((width, keys), LOW),
        pltpu.VMEM((keys, 8), F32),
        pltpu.VMEM((HEADS, TILE, LANES), LOW),
        pltpu.VMEM((HEADS, TILE, LANES), LOW),
        pltpu.VMEM((width, TILE), F32),
        pltpu.VMEM((keys, width), F32),
        pltpu.VMEM((keys, width), F32),
        pltpu.VMEM((keys // TILE, HEADS, TILE, TILE), F32),
        pltpu.VMEM((keys // TILE, HEADS, TILE, TILE), F32),
        pltpu.VMEM((HEADS, TILE), F32),
    ]


def attention_backward(plan, q, kv, d_context, lse, owner, key_owner, x, made, name):
    number, width = q.shape
    keys = kv.shape[0]
    in_specs = [
        rows_of(width),
        at_block((keys, width), 0, 0),
        at_block((keys, width), 0, 1),
        rows_of(width),
        pl.BlockSpec((HEADS, TILE), lambda i, *_: (0, i)),
    ] + owner_specs(keys)
    out_specs = [rows_of(width), whole((keys, width)), whole((keys, width))]
    out_shape = [shaped((number, width), LOW), shaped((keys, width), LOW), shaped((keys, width), LOW)]
    operands = [q, kv, kv, d_context, lse, owner, key_owner]
    scratch = attend_back_scratch(keys, width)
    if made:
        shape = (width // 16, 3, 16, width) if made == "units" else (3 * width, width)
        in_specs.append(whole(x.shape))
        operands.append(x)
        out_specs.append(whole(shape))
        out_shape.append(shaped(shape, LOW))
        scratch.append(pltpu.VMEM((number, width), LOW))
        if made == "rows":
            scratch.append(wide_scratch(width))
    return call(
        functools.partial(attention_back_kernel, made=made),
        (number // TILE,),
        in_specs,
        out_specs,
        out_shape,
        scratch,
        number * keys * width * 4 + (6 * number * width * width if made else 0),
        12 * number * width,
        name,
        room=52,
    )(plan, *operands)


def cross_back_kernel(plan, *refs, wanted, tiles):
    attention, refs = refs[:7], refs[7:]
    normed, inverse, d_above, memory, context = refs[:5]
    far = refs[5 : 5 + sources_of(wanted)]
    small, d_memory, d_sum, d_context, g_query, g_pair, g_out, sums, *refs = refs[5 + sources_of(wanted) :]
    scratch, refs = refs[:10], refs[10:]
    d_query, dk, dv, d_product, wkv, wq, wo, semaphores = refs
    dk_sum, dv_sum = scratch[5:7]
    loads = fetches(far, plan, wanted, (wkv, wq, wo), semaphores)
    i = pl.program_id(0)

    @pl.when(i == 0)
    def _():
        for load in loads:
            load.start()
        sums[...] = jnp.zeros_like(sums)

    @pl.when(i < tiles)
    def _():
        d_query[pl.ds(pl.multiple_of(i * TILE, TILE), TILE), :] = attend_back(plan, i, *attention, scratch)

    @pl.when(i == tiles)
    def _():
        dk[...] = dk_sum[...].astype(LOW)
        dv[...] = dv_sum[...].astype(LOW)
        for load in loads:
            load.wait()
        low = normed[...] * small[4:5, :] + small[5:6, :]
        g_query[...] = nn(low.T.astype(LOW), d_query[...]).astype(LOW)

    @pl.when(i >= tiles)
    def _():
        row = pl.multiple_of((i - tiles) * TILE, TILE)
        mine = pl.ds(row, TILE)
        wk, wv = block_of(wkv, 0, 2), block_of(wkv, 1, 2)
        d_memory[...] = nt(dk[mine, :], wk) + nt(dv[mine, :], wv)
        d_one = d_above[...] + nt(d_query[mine, :], wq[...])
        hat = normed[mine, :]
        sums[0:1, :] += jnp.sum(d_one * hat, axis=0, keepdims=True)
        sums[1:2, :] += jnp.sum(d_one, axis=0, keepdims=True)
        total = ln_backward(d_one, hat, inverse[:, 0:1], small[4:5, :])
        d_sum[...] = total
        place = lax.broadcasted_iota(jnp.int32, (TILE, 1), 0) + row
        live = (place < plan[2, 0]).astype(F32)
        product = (total * live).astype(LOW)
        d_product[mine, :] = product
        d_context[...] = nt(product, wo[...]).astype(LOW)

    @pl.when(i == tiles + 1)
    def _():
        put_block(g_pair, 0, nn(turned(memory[...]), dk[...]).astype(LOW))

    @pl.when(i == tiles + 2)
    def _():
        put_block(g_pair, 1, nn(turned(memory[...]), dv[...]).astype(LOW))

    @pl.when(i == 2 * tiles - 1)
    def _():
        g_out[...] = nn(turned(context[...]), d_product[...]).astype(LOW)


def cross_backward(plan, q, kv, d_context, lse, owner, key_owner, normed, inverse, d_above, memory, context, far,
                   wanted, small):
    number, width = normed.shape
    keys = kv.shape[0]
    tiles = number // TILE
    full = whole((number, width))

    def first_rows(columns):
        return pl.BlockSpec((TILE, columns), lambda i, *_: (jnp.minimum(i, tiles - 1), 0))

    def first_columns(rows):
        return pl.BlockSpec((rows, TILE), lambda i, *_: (0, jnp.minimum(i, tiles - 1)))

    def later_rows(columns):
        return pl.BlockSpec((TILE, columns), lambda i, *_: (jnp.maximum(i - tiles, 0), 0))

    return call(
        functools.partial(cross_back_kernel, wanted=wanted, tiles=tiles),
        (2 * tiles,),
        [first_rows(width), at_block((keys, width), 0, 0), at_block((keys, width), 0, 1), first_rows(width),
         first_columns(HEADS), first_columns(1), whole((1, keys)),
         full, later_rows(LANES), later_rows(width), whole(memory.shape), full]
        + [FAR] * sources_of(wanted)
        + [whole(small.shape)],
        [later_rows(width), later_rows(width), later_rows(width), whole((width, width)),
         whole((width // 16, 2, 16, width)), whole((width, width)), whole((8, width))],
        [shaped((number, width), F32), shaped((number, width), F32), shaped((number, width), LOW),
         shaped((width, width), LOW), shaped((width // 16, 2, 16, width), LOW), shaped((width, width), LOW),
         shaped((8, width), F32)],
        attend_back_scratch(keys, width)
        + [pltpu.VMEM((number, width), LOW), pltpu.VMEM((keys, width), LOW), pltpu.VMEM((keys, width), LOW),
           pltpu.VMEM((number, width), LOW)]
        + fetch_scratch(wanted, width),
        16 * number * width * width + number * keys * width * 4,
        24 * number * width,
        "cross_back",
        room=58,
    )(plan, q, kv, kv, d_context, lse, owner, key_owner, normed, inverse, d_above, memory, context,
      *far[: sources_of(wanted)], small)


def qkv_inputs_kernel(plan, *refs, masked, wanted):
    if masked:
        dq, dk, dv, d_above, flags, *refs = refs
        far = refs[: sources_of(wanted)]
        d_x, mask_sum, near, semaphores, blocks, wide = refs[sources_of(wanted) :]
    else:
        dq, dk, dv, d_above, *refs = refs
        far = refs[: sources_of(wanted)]
        d_x, near, semaphores, blocks = refs[sources_of(wanted) :]
    width = dq.shape[1]

    @pl.when(pl.program_id(0) == 0)
    def _():
        (load,) = fetches(far, plan, wanted, (near,), semaphores)
        load.start()
        load.wait()
        if masked:
            mask_sum[...] = jnp.zeros_like(mask_sum)
            spread(wide, near[...])
        for j in range(3):
            if masked:
                blocks[:, j * width : j * width + width] = third_rows(wide, j)
            else:
                blocks[:, j * width : j * width + width] = block_of(near, j, 3)

    pieces = jnp.concatenate([dq[...], dk[...], dv[...]], axis=1)
    total = nt(pieces, blocks[...])
    if masked:
        total = total + d_above[...]
        hit = column_of(flags[...]) == 1.0
        d_x[...] = jnp.where(hit, 0.0, total)
        mask_sum[0:1, :] += jnp.sum(jnp.where(hit, total, 0.0), axis=0, keepdims=True)
    else:
        d_x[...] = d_above[...]
        d_x[...] += total


def qkv_inputs(plan, dq, dk, dv, d_above, far, wanted, flags, name):
    number, width = dq.shape
    masked = flags is not None
    in_specs = [rows_of(width)] * 4
    out_specs = [rows_of(width)]
    out_shape = [shaped((number, width), F32)]
    operands = [dq, dk, dv, d_above]
    scratch = fetch_scratch(wanted, width) + [pltpu.VMEM((width, 3 * width), LOW)]
    if masked:
        in_specs.append(pl.BlockSpec((1, TILE), lambda i, *_: (0, i)))
        out_specs.append(whole((8, width)))
        out_shape.append(shaped((8, width), F32))
        operands.append(flags)
        scratch.append(wide_scratch(width))
    in_specs += [FAR] * sources_of(wanted)
    operands += far[: sources_of(wanted)]
    return call(
        functools.partial(qkv_inputs_kernel, masked=masked, wanted=wanted),
        (number // TILE,),
        in_specs,
        out_specs,
        out_shape,
        scratch,
        6 * number * width * width,
        16 * number * width,
        name,
    )(plan, *operands)


def enc_regions(width, inner):
    return ((0, 3 * width, 3), (4 * width, 4 * width + inner, inner // width))


def dec_regions(width, inner):
    return ((5 * width, 7 * width, 2), (8 * width, 8 * width + inner, inner // width))


def to_units(rows, k):
    return rows.reshape(-1, 16, k, rows.shape[1]).transpose(0, 2, 1, 3).reshape(rows.shape)


def from_units(rows, k):
    return rows.reshape(-1, k, 16, rows.shape[1]).transpose(0, 2, 1, 3).reshape(rows.shape)


def fits(size, region):
    return size % (16 * region[2]) == 0


def arrange_own(rows, first, regions, arrange):
    place = first + lax.broadcasted_iota(jnp.int32, (rows.shape[0], 1), 0)
    result = rows
    for region in regions:
        if fits(rows.shape[0], region):
            inside = (place >= region[0]) & (place < region[1])
            result = jnp.where(inside, arrange(rows, region[2]), result)
    return result


def arrange_all(rows, size, regions, arrange):
    for region in regions:
        if not fits(size, region):
            part = arrange(rows[region[0] : region[1]], region[2])
            rows = jnp.concatenate([rows[: region[0]], part, rows[region[1] :]], axis=0)
    return rows


def owners_of(lengths, number):
    bounds = jnp.cumsum(lengths)
    places = jnp.arange(number, dtype=jnp.int32)
    owners = jnp.sum((places[:, None] >= bounds[None, :]).astype(jnp.int32), axis=1)
    filled = places < bounds[-1]
    for_queries = jnp.where(filled, owners, -2).astype(F32)[None, :]
    for_keys = jnp.where(filled, owners, -1).astype(F32)[None, :]
    return for_queries, for_keys, bounds


def plan_of(query_bounds, key_bounds, key_lengths, number, core):
    firsts = jnp.arange(8, dtype=jnp.int32) * TILE
    filled = query_bounds[-1]
    lasts = jnp.minimum(firsts + TILE, filled) - 1

    def pair_of(places):
        found = jnp.sum((places[:, None] >= query_bounds[None, :]).astype(jnp.int32), axis=1)
        return jnp.minimum(found, key_lengths.shape[0] - 1)

    def pick(values, pairs):
        chosen = pairs[:, None] == jnp.arange(values.shape[0])[None, :]
        return jnp.sum(jnp.where(chosen, values[None, :], 0), axis=1)

    begin = pick(key_bounds - key_lengths, pair_of(firsts))
    end = pick(key_bounds, pair_of(lasts))
    some = firsts < filled
    begin = begin // LANES * LANES
    chunks = (end - begin + TILE - 1) // TILE
    begin = jnp.where(some, jnp.minimum(begin, number - chunks * TILE), 0)
    chunks = jnp.where(some, chunks, 0)
    rest = jnp.where(jnp.arange(8) == 1, core, filled)
    return jnp.stack([begin, chunks, rest]).astype(jnp.int32)


def moments(gradient, first, second):
    first_new = beta_one * first + (1.0 - beta_one) * gradient
    second_new = beta_two * second + (1.0 - beta_two) * gradient * gradient
    return (first_new, second_new)


def adamw(weight, gradient, first, second):
    first_new, second_new = moments(gradient, first, second)
    moved = weight - rate * (
        first_new
        / (1.0 - beta_one**STEPS)
        / (jnp.sqrt(second_new / (1.0 - beta_two**STEPS)) + epsilon)
        + decay * weight
    )
    return (moved, first_new, second_new)


CORE, X, Y, Z_LOW, Z_HIGH = 0, 1, 2, 3, 4
BITS = 5


def partner(bits):
    mask = sum(1 << bit for bit in bits)
    return [(i, i ^ mask) for i in range(1 << BITS)]


def bit_of(me, bit):
    return (me >> bit) & 1


def take(values, axis, index):
    return lax.dynamic_index_in_dim(values, index, axis, keepdims=False)


def overlaps(sizes, own):
    found = []
    first = 0
    for piece, size in enumerate(sizes):
        at = first
        while at < first + size:
            owner = at // own
            end = min(first + size, (owner + 1) * own)
            found.append((piece, at - first, owner, at - owner * own, end - at))
            at = end
        first += size
    return found


def pack_kernel(core, *refs, copies, number):
    pieces, send, keep, semaphores = refs[:number], refs[number], refs[number + 1], refs[number + 2]
    for side in (0, 1):

        @pl.when(core[0] == side)
        def _():
            handles = []
            for n, (piece, at, owner, to, rows) in enumerate(copies):
                target = keep if owner % 2 == side else send
                handles.append(
                    pltpu.make_async_copy(
                        pieces[piece].at[pl.ds(at, rows)],
                        target.at[owner // 2, pl.ds(to, rows)],
                        semaphores.at[n],
                    )
                )
            for handle in handles:
                handle.start()
            for handle in handles:
                handle.wait()


def pack(core, pieces, copies, block, name):
    width = pieces[0].shape[1]
    shape = shaped((1 << (BITS - 1), block, width), LOW)
    anywhere = pl.BlockSpec(memory_space=pl.ANY)
    total = sum(piece.size for piece in pieces)
    return call(
        functools.partial(pack_kernel, copies=copies, number=len(pieces)),
        (1,),
        [pl.BlockSpec(memory_space=pltpu.VMEM)] * len(pieces),
        [anywhere, anywhere],
        [shape, shape],
        [pltpu.SemaphoreType.DMA((len(copies),))],
        0,
        4 * total,
        name,
        near=True,
    )(core, *pieces)


def add_low(former, latter):
    return (former.astype(F32) + latter.astype(F32)).astype(LOW)


def swap(values, *bits):
    return lax.ppermute(values, "fsdp", partner(bits))


def reduce_owned(me, send, keep, cut):
    rows, width = send.shape[1:]
    x, y, low, high = (bit_of(me, b) for b in (X, Y, Z_LOW, Z_HIGH))
    (send,) = yield (send,)
    chips = add_low(keep, swap(send, CORE)).reshape(2, 2, 2, 2, rows, width)
    first, second = chips[..., :cut, :], chips[..., cut:, :]
    for_y, for_x = yield (take(first, 2, 1 - y), take(second, 3, 1 - x))
    first = add_low(take(first, 2, y), swap(for_y, Y))
    second = add_low(take(second, 3, x), swap(for_x, X))
    for_x, for_y = yield (take(first, 2, 1 - x), take(second, 2, 1 - y))
    first = add_low(take(first, 2, x), swap(for_x, X))
    second = add_low(take(second, 2, y), swap(for_y, Y))
    column = jnp.concatenate([first, second], axis=2)

    def block(above, beside):
        return take(take(column, 0, above), 0, beside)

    near, far, across = yield (block(high, 1 - low), block(1 - high, low), block(1 - high, 1 - low))
    total = block(high, low).astype(F32)
    for values, bits in ((near, (Z_LOW,)), (far, (Z_HIGH,)), (across, (Z_LOW, Z_HIGH))):
        total = total + swap(values, *bits).astype(F32)
    return total


def ordered(bit, mine, other, axis):
    first = bit == 0
    return jnp.stack([jnp.where(first, mine, other), jnp.where(first, other, mine)], axis=axis)


def gather_owned(me, own):
    x, y, low, high = (bit_of(me, b) for b in (X, Y, Z_LOW, Z_HIGH))
    rows, width = own.shape
    (own,) = yield (own,)
    column = ordered(high, own, swap(own, Z_HIGH), 0)
    (column,) = yield (column,)
    column = ordered(low, column, swap(column, Z_LOW), 1)
    below, above = yield (column[0], column[1])
    below = ordered(x, below, swap(below, X), 1)
    above = ordered(y, above, swap(above, Y), 1)
    below, above = yield (below, above)
    below = ordered(y, below, swap(below, Y), 1).reshape(-1, rows, width)
    above = ordered(x, above, swap(above, X), 2).reshape(-1, rows, width)
    below, above = yield (below, above)
    return [below, swap(below, CORE), above, swap(above, CORE)]


class Rounds:
    def __init__(self, steps):
        self.steps = steps
        self.sent = next(steps)
        self.result = None

    def before(self, *operands):
        sent, operands = lax.optimization_barrier((self.sent, operands))
        self.move(sent)
        return operands[0] if len(operands) == 1 else operands

    def move(self, sent):
        try:
            self.sent = self.steps.send(sent)
        except StopIteration as stop:
            self.sent, self.result = None, stop.value

    def finish(self):
        while self.result is None:
            self.move(self.sent)
        return self.result


def on_device(
    devices,
    src_in,
    tgt_in,
    src_len,
    tgt_len,
    tgt_mask,
    enc_cot,
    dec_cot,
    enc_master,
    enc_first,
    enc_second,
    dec_master,
    dec_first,
    dec_second,
    small_master,
    small_first,
    small_second,
):
    width = src_in.shape[1]
    number = src_in.shape[0]
    me = lax.axis_index("fsdp")
    enc_size, dec_size = enc_master.shape[0], dec_master.shape[0]
    enc_count, dec_count = enc_size * devices, dec_size * devices
    inner = (enc_count - 4 * width) // 2
    ups = inner // width
    enc_map, dec_map = enc_regions(width, inner), dec_regions(width, inner)

    enc_own = arrange_own(enc_master.astype(LOW), me * enc_size, enc_map, to_units)
    dec_own = arrange_own(dec_master.astype(LOW), me * dec_size, dec_map, to_units)
    by_rounds = devices == 1 << BITS
    share = small_master.shape[1]
    held = small_master.size
    own = jnp.zeros((16, width), LOW)
    own = lax.dynamic_update_slice(own, small_master.astype(LOW), (0, me * share))
    core = bit_of(me, CORE)
    src_owner, src_key, src_bounds = owners_of(src_len[0], number)
    tgt_owner, tgt_key, tgt_bounds = owners_of(tgt_len[0], number)
    enc_plan = plan_of(src_bounds, src_bounds, src_len[0], number, core)
    dec_plan = plan_of(tgt_bounds, tgt_bounds, tgt_len[0], number, core)
    cross_plan = plan_of(tgt_bounds, src_bounds, src_len[0], number, core)
    flags = tgt_mask.astype(F32)[None, :]
    if by_rounds:
        ahead = Rounds(gather_owned(me, jnp.concatenate([enc_own, own], axis=0)))
        ahead.move(ahead.sent)
        ahead.move(ahead.sent)
        dec_own = ahead.before(dec_own)
        behind = Rounds(gather_owned(me, dec_own))
        behind.move(behind.sent)
        behind.sent = (ahead.before(*behind.sent),)
        behind.move(behind.sent)
        ahead.sent, behind.sent = lax.optimization_barrier((ahead.sent, behind.sent))
        behind.move(behind.sent)
        ahead.sent, behind.sent = lax.optimization_barrier((ahead.sent, behind.sent))
        enc_far, behind.sent = lax.optimization_barrier((ahead.finish(), behind.sent))
        smalls = sum(jnp.sum(part[:, enc_size:].astype(F32), axis=0) for part in enc_far)
        early = (src_in, src_owner, src_key, tgt_owner, tgt_key, enc_plan, dec_plan, cross_plan, flags)
        src_in, src_owner, src_key, tgt_owner, tgt_key, enc_plan, dec_plan, cross_plan, flags = behind.before(*early)
    else:
        first = core == 0

        def paired(own_rows, size, regions):
            rows = lax.all_gather(own_rows, "fsdp", axis=0, tiled=True)
            rows = arrange_all(rows, size, regions, to_units).reshape(2, OWNERS // 4, 2, -1, width)
            made = []
            for half in range(2):
                even, odd = rows[half, :, 0], rows[half, :, 1]
                made += [jnp.where(first, even, odd), jnp.where(first, odd, even)]
            return made

        enc_far, dec_far = paired(enc_own, enc_size, enc_map), paired(dec_own, dec_size, dec_map)
        smalls = lax.psum(own.astype(F32), "fsdp")

    def enc_part(first, last):
        return row_copies(first, last, enc_count // OWNERS, True)

    def dec_part(first, last):
        return row_copies(first, last, dec_count // OWNERS, True)

    enc_qkv = enc_part(0, 3 * width)
    enc_wo = enc_part(3 * width, 4 * width)
    enc_up = enc_part(4 * width, 4 * width + inner)
    enc_down = enc_part(4 * width + inner, enc_count)
    self_qkv = dec_part(0, 3 * width)
    self_wo = dec_part(3 * width, 4 * width)
    cross_q = dec_part(4 * width, 5 * width)
    cross_kv = dec_part(5 * width, 7 * width)
    cross_wo = dec_part(7 * width, 8 * width)
    dec_up = dec_part(8 * width, 8 * width + inner)
    dec_down = dec_part(8 * width + inner, dec_count)

    start = jnp.where(tgt_mask[:, None] == 1, smalls[10].astype(LOW)[None, :], tgt_in)

    e_q, e_kv, e_ctx, e_lse, e_hat, e_inv, memory, t_hat, t_inv = fwd_block(
        enc_plan, src_in, None, enc_far, (enc_qkv, enc_wo, enc_up, enc_down), True, smalls, 0, src_owner, src_key, True,
        "enc_layer",
    )
    if by_rounds:
        memory = behind.before(memory)
        dec_far = behind.finish()
    s_q, s_kv, s_ctx, s_lse, s_hat, s_inv = fwd_block(
        dec_plan, start, None, dec_far, (self_qkv, self_wo), False, smalls, 4, tgt_owner, tgt_key, False, "dec_block"
    )
    c_q, c_kv, c_lse, decoded, d_two, d_cctx, g_dup, g_ddown, g_cout, sums_d = cross_turn(
        cross_plan, s_hat, memory, dec_cot, dec_far, (cross_kv, cross_wo, cross_q, dec_up, dec_down), smalls, 6,
        tgt_owner, src_key, inner, "cross_turn",
    )

    d_memory, d_one, d_sctx, g_cq, g_ckv, g_sout, sums_c = cross_backward(
        cross_plan, c_q, c_kv, d_cctx, c_lse, tgt_owner, src_key, s_hat, s_inv, d_two, memory, s_ctx, dec_far,
        (cross_kv, cross_q, self_wo), smalls,
    )
    dsq, dsk, dsv, g_sqkv = attention_backward(
        dec_plan, s_q, s_kv, d_sctx, s_lse, tgt_owner, tgt_key, start, "rows", "dec_back"
    )
    dec_pieces = [
        g_sqkv,
        g_sout,
        g_cq,
        g_ckv.reshape(-1, width),
        g_cout,
        g_dup.reshape(-1, width),
        g_ddown,
    ]
    if by_rounds:
        core = core[None].astype(jnp.int32)
        copies = overlaps([p.shape[0] for p in dec_pieces], dec_size)
        send, keep = pack(core, dec_pieces, copies, dec_size, "dec_pack")
        rounds = Rounds(reduce_owned(me, send, keep, dec_size // 2))
        dsq, dsk, dsv = rounds.before(dsq, dsk, dsv)
    tgt_grad, mask_sum = qkv_inputs(
        dec_plan, dsq, dsk, dsv, d_one, dec_far, (self_qkv,), flags, "dec_qkv_inputs"
    )
    if by_rounds:
        d_memory, mask_sum = rounds.before(d_memory, mask_sum)
    d_mid, d_ectx, g_up, g_down, g_out, sums_e = ffn_backward(
        enc_plan, [enc_cot, d_memory], (t_hat, t_inv), (e_hat, e_inv), e_ctx, enc_far,
        (enc_up, enc_down, enc_wo), smalls, 0, inner, "enc_ffn_back",
    )
    if by_rounds:
        d_ectx, g_up = rounds.before(d_ectx, g_up)
    deq, dek, dev, g_qkv = attention_backward(
        enc_plan, e_q, e_kv, d_ectx, e_lse, src_owner, src_key, src_in, "units", "enc_back"
    )

    enc_pieces = [g_qkv.reshape(-1, width), g_out, g_up.reshape(-1, width), g_down]
    small_grad = jnp.concatenate([sums_e[:4], sums_c[:2], sums_d[:4], mask_sum[:1]], axis=0)
    small_wire = small_grad.reshape(-1, devices, share).transpose(1, 0, 2).reshape(devices, -1).astype(LOW)
    small_wire = jnp.pad(small_wire, ((0, 0), (0, 16 * width - held))).reshape(devices * 16, width)
    if by_rounds:
        dec_summed = rounds.finish()
        copies = overlaps([p.shape[0] for p in enc_pieces], enc_size)
        copies += [(len(enc_pieces), 16 * i, i, enc_size, 16) for i in range(devices)]
        send, keep = pack(core, enc_pieces + [small_wire], copies, enc_size + 16, "enc_pack")
        rounds = Rounds(reduce_owned(me, send, keep, enc_size // 2 + 16))
        deq, dek, dev = rounds.before(deq, dek, dev)
    src_grad = qkv_inputs(enc_plan, deq, dek, dev, d_mid, enc_far, (enc_qkv,), None, "enc_qkv_inputs")[0]
    if by_rounds:
        rounds.move(rounds.sent)
        rounds.move(rounds.sent)
        dec_summed = rounds.before(dec_summed)
        enc_summed = rounds.finish()
    else:
        dec_grad = arrange_all(jnp.concatenate(dec_pieces, axis=0), dec_size, dec_map, from_units)
        enc_grad = arrange_all(jnp.concatenate(enc_pieces, axis=0), enc_size, enc_map, from_units)
        enc_wire = jnp.concatenate(
            [enc_grad.reshape(devices, enc_size, width), small_wire.reshape(devices, 16, width)], axis=1
        )
        dec_summed = lax.psum_scatter(dec_grad, "fsdp", scatter_dimension=0, tiled=True).astype(F32)
        enc_summed = lax.psum_scatter(
            enc_wire.reshape(-1, width), "fsdp", scatter_dimension=0, tiled=True
        ).astype(F32)
    small_summed = enc_summed[enc_size:].reshape(-1)[:held].reshape(-1, share)
    enc_summed = arrange_own(enc_summed[:enc_size], me * enc_size, enc_map, from_units)
    dec_summed = arrange_own(dec_summed, me * dec_size, dec_map, from_units)

    part = 1.0 / devices
    enc_summed = enc_summed * part
    dec_summed = dec_summed * part
    small_summed = small_summed * part
    enc_new, enc_first_new, encoder_second_moment_updated = adamw(
        enc_master, enc_summed, enc_first, enc_second
    )
    dec_new, dec_first_new, dec_second_new = adamw(dec_master, dec_summed, dec_first, dec_second)
    small_first_new, small_second_new = moments(small_summed, small_first, small_second)
    return (
        memory,
        decoded,
        src_grad,
        tgt_grad,
        enc_new,
        enc_first_new,
        encoder_second_moment_updated,
        enc_new.astype(LOW),
        dec_new,
        dec_first_new,
        dec_second_new,
        dec_new.astype(LOW),
        small_summed,
        small_first_new,
        small_second_new,
    )


def solution(mesh):
    rows = P("fsdp", None)
    columns = P(None, "fsdp")
    return jax.shard_map(
        functools.partial(on_device, mesh.shape["fsdp"]),
        mesh=mesh,
        in_specs=(rows,) * 4 + (P("fsdp"),) + (rows,) * 8 + (columns,) * 3,
        out_specs=(rows,) * 12 + (columns,) * 3,
        check_vma=False,
    )
```

profile of v0, /device:TPU:0, one launch (start us, length us, event | category | flops | bytes accessed | tf_op | source)
XLA Modules:
  0.0 404.3 jit_solution(8652736770781429859)
XLA Ops:
  0.7 1.1 convert_element_type.248
  3.4 4.1 %collective-permute-start = (bf16[208,512]{1,0:T(8,128)(2,1)S(1)}, bf16[208,512]{1,0:T(8,128)(2,1)S(1)}, u32[]{:S(2)}, u32[]{:S(2)}) collective-permute-start(bf16[208,512]{1,0:T(8,128)(2,1)S(1)} %pad_maximum_fusion.12), channel_id=1, source_target_pairs={{0,16},{1,17},{2,18},{3,19},{4,20},{5,21},{6,22},{7,23},{8,24},{9,... | collective-permute-start | bytes 638984 | tf_op jit(solution)/shard_map/ppermute | solution.py:1203
  8.1 9.4 %collective-permute-done = bf16[208,512]{1,0:T(8,128)(2,1)S(1)} collective-permute-done((bf16[208,512]{1,0:T(8,128)(2,1)S(1)}, bf16[208,512]{1,0:T(8,128)(2,1)S(1)}, u32[]{:S(2)}, u32[]{:S(2)}) %collective-permute-start) | collective-permute-done | bytes 213024 | tf_op jit(solution)/shard_map/ppermute | solution.py:1203
  20.0 9.1 %collective-permute-done.1 = bf16[2,208,512]{2,1,0:T(8,128)(2,1)S(1)} collective-permute-done((bf16[2,208,512]{2,1,0:T(8,128)(2,1)S(1)}, bf16[2,208,512]{2,1,0:T(8,128)(2,1)S(1)}, u32[]{:S(2)}, u32[]{:S(2)}) %collective-permute-start.1) | collective-permute-done | bytes 426016 | tf_op jit(solution)/shard_map/ppermute | solution.py:1203
  29.3 2.9 collective-permute-start.4
  32.1 1.5 collective-permute-start.2
  34.4 1.6 collective-permute-start.3
  36.0 7.8 %collective-permute-done.4 = bf16[256,512]{1,0:T(8,128)(2,1)S(1)} collective-permute-done((bf16[256,512]{1,0:T(8,128)(2,1)S(1)}, bf16[256,512]{1,0:T(8,128)(2,1)S(1)}, u32[]{:S(2)}, u32[]{:S(2)}) %collective-permute-start.4) | collective-permute-done | bytes 262176 | tf_op jit(solution)/shard_map/ppermute | solution.py:1203
  44.0 1.1 collective-permute-done.3
  45.2 1.5 collective-permute-start.7
  47.4 1.6 collective-permute-start.5
  50.0 7.2 %collective-permute-done.7 = bf16[2,256,512]{2,1,0:T(8,128)(2,1)S(1)} collective-permute-done((bf16[2,256,512]{2,1,0:T(8,128)(2,1)S(1)}, bf16[2,256,512]{2,1,0:T(8,128)(2,1)S(1)}, u32[]{:S(2)}, u32[]{:S(2)}) %collective-permute-start.7) | collective-permute-done | bytes 524320 | tf_op jit(solution)/shard_map/ppermute | solution.py:1203
  57.3 8.8 %collective-permute-done.5 = bf16[2,2,208,512]{3,2,0,1:T(8,128)(2,1)S(1)} collective-permute-done((bf16[2,2,208,512]{3,2,0,1:T(8,128)(2,1)S(1)}, bf16[2,2,208,512]{3,2,0,1:T(8,128)(2,1)S(1)}, u32[]{:S(2)}, u32[]{:S(2)}) %collective-permute-start.5) | collective-permute-done | bytes 852000 | tf_op jit(solution)/shard_map/ppermute | solution.py:1203
  66.7 1.2 collective-permute-done.6
  68.3 1.6 collective-permute-start.8
  71.1 8.5 %collective-permute-done.8 = bf16[2,256,512]{2,1,0:T(8,128)(2,1)S(1)} collective-permute-done((bf16[2,256,512]{2,1,0:T(8,128)(2,1)S(1)}, bf16[2,256,512]{2,1,0:T(8,128)(2,1)S(1)}, u32[]{:S(2)}, u32[]{:S(2)}) %collective-permute-start.8) | collective-permute-done | bytes 524320 | tf_op jit(solution)/shard_map/ppermute | solution.py:1203
  79.8 1.3 collective-permute-done.9
  85.4 1.9 fusion.35
  89.2 24.4 %enc_layer.1 = (bf16[1024,512]{1,0:T(8,128)(2,1)}, bf16[1024,1024]{1,0:T(8,128)(2,1)}, bf16[1024,512]{1,0:T(8,128)(2,1)}, f32[8,1024]{1,0:T(8,128)}, f32[1024,51...) custom-call(s32[3,8]{1,0:T(4,128)S(1)} %pad_add_fusion.2.plan, ...), custom_call_target="tpu_custom_call" | custom-call | flops 3221225472 | bytes 8388608 | tf_op jit(solution)/shard_map/enc_layer/pallas_call | solution.py:224
  117.0 1.2 broadcast_select_fusion.refs_0_.refs_7_
  118.2 1.8 collective-permute-done.14.refs_2_.refs_4_.refs_13_.refs_6_
  120.1 1.3 copy-done.19
  121.4 18.8 %dec_block.1 = (bf16[1024,512]{1,0:T(8,128)(2,1)}, bf16[1024,1024]{1,0:T(8,128)(2,1)}, bf16[1024,512]{1,0:T(8,128)(2,1)}, f32[8,1024]{1,0:T(8,128)}, f32[1024,512]{1,0:T(8,128)}, /*index=5*/f32[1024,128]{1,0:T(8,128)}) custom-call(s32[3,8]{1,0:T(4,128)S(1)} %get-tuple-element.150.plan, bf16[1024,512]{1,0:T(8,128)(2,1)} %broadcast_select_fusion.refs_0_.refs_7_, ...), custom_call_target="tpu_custom_call" | custom-call | flops 3221225472 | bytes 8388608 | tf_op jit(solution)/shard_map/dec_block/pallas_call | solution.py:224
  140.3 1.3 copy-done.38
  141.6 41.8 %cross_turn.1 = (bf16[1024,512]{1,0:T(8,128)(2,1)}, bf16[1024,1024]{1,0:T(8,128)(2,1)}, f32[8,1024]{1,0:T(8,128)}, bf16[1024,512]{1,0:T(8,128)(2,1)}, f32[1024,5...) custom-call(s32[3,8]{1,0:T(4,128)} %get-tuple-element.149.plan, ...), custom_call_target="tpu_custom_call" | custom-call | flops 13958643712 | bytes 15728640 | tf_op jit(solution)/shard_map/cross_turn/pallas_call | solution.py:224
  183.5 28.7 %cross_back.1 = (f32[1024,512]{1,0:T(8,128)}, f32[1024,512]{1,0:T(8,128)}, bf16[1024,512]{1,0:T(8,128)(2,1)}, bf16[512,512]{1,0:T(8,128)(2,1)}, bf16[32,2,16,512...) custom-call(s32[3,8]{1,0:T(4,128)} %get-tuple-element.149.plan, ...), custom_call_target="tpu_custom_call" | custom-call | flops 6442450944 | bytes 12582912 | tf_op jit(solution)/shard_map/cross_back/pallas_call | solution.py:224
  212.2 23.2 %dec_back.1 = (bf16[1024,512]{1,0:T(8,128)(2,1)}, bf16[1024,512]{1,0:T(8,128)(2,1)}, bf16[1024,512]{1,0:T(8,128)(2,1)}, bf16[1536,512]{1,0:T(8,128)(2,1)}) custom-call(s32[3,8]{1,0:T(4,128)S(1)} %get-tuple-element.150.plan, bf16[1024,512]{1,0:T(8,128)(2,1)} %get-tuple-element.159.refs_0_, bf16[1024,1024]{1,0:T(8,128)(2,1)} %get-tuple-element.160.refs_1_.refs_2_, ...), custom_call_target="tpu_custom_call" | custom-call | flops 3758096384 | bytes 6291456 | tf_op jit(solution)/shard_map/dec_back/pallas_call | solution.py:224
  235.5 1.4 copy-done.4
  236.9 3.6 dec_pack.1
  242.0 8.7 %dec_qkv_inputs.1 = (f32[1024,512]{1,0:T(8,128)}, f32[8,512]{1,0:T(8,128)}) custom-call(s32[3,8]{1,0:T(4,128)S(1)} %get-tuple-element.150.plan, bf16[1024,512]{1,0:T(8,128)(2,1)} %get-tuple-element.184.refs_0_, bf16[1024,512]{1,0:T(8,128)(2,1)} %get-tuple-element.185.refs_1_, bf16[1024,512]{1,0:T(8,128)(2,1)} %get-tuple-element.186.refs_2_, ...), custom_call_target="tpu_custom_call" | custom-call | flops 1610612736 | bytes 8388608 | tf_op jit(solution)/shard_map/dec_qkv_inputs/pallas_call | solution.py:224
  250.7 3.6 add_convert_fusion
  254.9 1.1 copy.139
  256.2 1.1 copy.140
  258.0 5.3 %collective-permute-start.17 = (bf16[2,2,2,128,512]{4,3,1,0,2:T(8,128)(2,1)}, bf16[2,2,2,128,512]{4,3,1,0,2:T(8,128)(2,1)}, u32[]{:S(2)}, u32[]{:S(2)}) collective-permute-start(bf16[2,2,2,128,512]{4,3,1,0,2:T(8,128)(2,1)} %bitcast.273), channel_id=1, source_target_pairs={{0,4},{1,5},{2,6},{3,7},{4,0},{5,1},{6,2},{7,3},{8,12},{9,13},{10,... | collective-permute-start | bytes 3145736 | tf_op jit(solution)/shard_map/ppermute | solution.py:1203
  263.3 26.5 %enc_ffn_back.1 = (f32[1024,512]{1,0:T(8,128)}, bf16[1024,512]{1,0:T(8,128)(2,1)}, bf16[32,4,16,512]{3,2,1,0:T(8,128)(2,1)}, bf16[2048,512]{1,0:T(8,128)(2,1)}, ...) custom-call(s32[3,8]{1,0:T(4,128)S(1)} %pad_add_fusion.2.plan, bf16[1024,512]{1,0:T(8,128)(2,1)} %refs_0_.2, ...), custom_call_target="tpu_custom_call" | custom-call | flops 10737418240 | bytes 15728640 | tf_op jit(solution)/shard_map/enc_ffn_back/pallas_call | solution.py:224
  290.9 0.9 pad.4.clone
  291.8 1.3 reshape.741.refs_4_
  293.0 1.5 fusion.1
  294.6 0.9 dynamic-slice_bitcast_fusion.1
  295.5 1.5 fusion
  297.9 20.2 %enc_back.1 = (bf16[1024,512]{1,0:T(8,128)(2,1)}, bf16[1024,512]{1,0:T(8,128)(2,1)}, bf16[1024,512]{1,0:T(8,128)(2,1)}, bf16[32,3,16,512]{3,2,1,0:T(8,128)(2,1)}) custom-call(s32[3,8]{1,0:T(4,128)S(1)} %pad_add_fusion.2.plan, bf16[1024,512]{1,0:T(8,128)(2,1)} %get-tuple-element.157.refs_0_, bf16[1024,1024]{1,0:T(8,128)(2,1)} %get-tuple-element.158.refs_1_.refs_2_, ...), custom_call_target="tpu_custom_call" | custom-call | flops 3758096384 | bytes 6291456 | tf_op jit(solution)/shard_map/enc_back/pallas_call | solution.py:224
  318.1 1.4 copy-done.5
  319.5 3.3 enc_pack.1
  322.9 1.8 collective-permute-start.19
  324.7 1.9 collective-permute-start.24
  326.7 8.0 %enc_qkv_inputs.1 = f32[1024,512]{1,0:T(8,128)} custom-call(s32[3,8]{1,0:T(4,128)S(1)} %pad_add_fusion.2.plan, bf16[1024,512]{1,0:T(8,128)(2,1)} %get-tuple-element.214.refs_0_, bf16[1024,512]{1,0:T(8,128)(2,1)} %get-tuple-element.215.refs_1_, bf16[1024,512]{1,0:T(8,128)(2,1)} %get-tuple-element.216.refs_2_, f32[1024,512]{1,0:T(8,128)} %get-tuple-element.217.refs_3_, ...), custom_call_target="tpu_custom_call" | custom-call | flops 1610612736 | bytes 8388608 | tf_op jit(solution)/shard_map/enc_qkv_inputs/pallas_call | solution.py:224
  334.7 3.1 add_convert_fusion.1
  338.4 1.9 collective-permute-start.22
  341.2 2.0 collective-permute-start.26
  343.2 9.4 %collective-permute-start.27 = (bf16[256,512]{1,0:T(8,128)(2,1)S(1)}, bf16[256,512]{1,0:T(8,128)(2,1)S(1)}, u32[]{:S(2)}, u32[]{:S(2)}) collective-permute-start(bf16[256,512]{1,0:T(8,128)(2,1)S(1)} %get-tuple-element.264), channel_id=1, source_target_pairs={{0,16},{1,17},{2,18},{3,19},{4,20},{5,21},{6,22},{7,23},{8,24},{9,... | collective-permute-start | bytes 786440 | tf_op jit(solution)/shard_map/ppermute | solution.py:1203
  352.5 1.4 collective-permute-start.28
  353.9 4.0 collective-permute-done.22
  358.2 1.8 collective-permute-start.23
  360.0 3.9 collective-permute-done.20
  364.4 6.6 %collective-permute-done.27 = bf16[256,512]{1,0:T(8,128)(2,1)S(1)} collective-permute-done((bf16[256,512]{1,0:T(8,128)(2,1)S(1)}, bf16[256,512]{1,0:T(8,128)(2,1)S(1)}, u32[]{:S(2)}, u32[]{:S(2)}) %collective-permute-start.27) | collective-permute-done | bytes 262176 | tf_op jit(solution)/shard_map/ppermute | solution.py:1203
  371.3 2.0 collective-permute-done.21
  374.2 2.9 collective-permute-start.29
  377.2 7.7 %collective-permute-start.30 = (bf16[208,512]{1,0:T(8,128)(2,1)}, bf16[208,512]{1,0:T(8,128)(2,1)}, u32[]{:S(2)}, u32[]{:S(2)}) collective-permute-start(bf16[208,512]{1,0:T(8,128)(2,1)} %get-tuple-element.224), channel_id=1, source_target_pairs={{0,16},{1,17},{2,18},{3,19},{4,20},{5,21},{6,22},{7,23},{8,24},{9,... | collective-permute-start | bytes 638984 | tf_op jit(solution)/shard_map/ppermute | solution.py:1203
  384.9 1.5 collective-permute-start.31
  387.3 1.2 reshape.750
  388.5 3.1 fusion.48
  391.6 7.8 %collective-permute-done.30 = bf16[208,512]{1,0:T(8,128)(2,1)} collective-permute-done((bf16[208,512]{1,0:T(8,128)(2,1)}, bf16[208,512]{1,0:T(8,128)(2,1)}, u32[]{:S(2)}, u32[]{:S(2)}) %collective-permute-start.30) | collective-permute-done | bytes 213024 | tf_op jit(solution)/shard_map/ppermute | solution.py:1203
  399.4 1.1 fusion.17
  402.3 1.5 fusion.49
  (227 shorter events, 30.6 us)
Async XLA Ops:
  0.6 2.6 copy-start.17
  0.7 6.8 %copy-start.36 = (s32[1,16]{1,0:T(1,128)S(1)}, s32[1,16]{1,0:T(1,128)}, u32[]{:S(2)}) copy-start(s32[1,16]{1,0:T(1,128)} %param.19) | copy-start | bytes 196
  1.9 17.4 %copy-start.13 = (f32[256,512]{1,0:T(8,128)S(1)}, f32[256,512]{1,0:T(8,128)}, u32[]{:S(2)}) copy-start(f32[256,512]{1,0:T(8,128)} %param.26) | copy-start | bytes 1572868
  2.0 17.2 %copy-start.30 = (pred[192]{0:T(512)(128)(4,1)}, pred[192]{0:T(512)(128)(4,1)S(1)}, u32[]{:S(2)}) copy-start(pred[192]{0:T(512)(128)(4,1)S(1)} %get-tuple-element.304) | copy-start | bytes 580
  2.0 17.2 %copy-start.32 = (pred[192]{0:T(512)(128)(4,1)}, pred[192]{0:T(512)(128)(4,1)S(1)}, u32[]{:S(2)}) copy-start(pred[192]{0:T(512)(128)(4,1)S(1)} %get-tuple-element.305) | copy-start | bytes 580
  3.4 14.2 %collective-permute-start = (bf16[208,512]{1,0:T(8,128)(2,1)S(1)}, bf16[208,512]{1,0:T(8,128)(2,1)S(1)}, u32[]{:S(2)}, u32[]{:S(2)}) collective-permute-start(bf16[208,512]{1,0:T(8,128)(2,1)S(1)} %pad_maximum_fusion.12), channel_id=1, source_target_pairs={{0,16},{1,17},{2,18},{3,19},{4,20},{5,21},{6,22},{7,23},{8,24},{9,... | collective-permute-start | bytes 638984 | tf_op jit(solution)/shard_map/ppermute | solution.py:1203
  8.1 11.7 %copy-start.34 = (pred[256]{0:T(512)(128)(4,1)}, pred[256]{0:T(512)(128)(4,1)S(1)}, u32[]{:S(2)}) copy-start(pred[256]{0:T(512)(128)(4,1)S(1)} %get-tuple-element.306) | copy-start | bytes 772
  8.1 11.7 %copy-start.35 = (pred[256]{0:T(512)(128)(4,1)}, pred[256]{0:T(512)(128)(4,1)S(1)}, u32[]{:S(2)}) copy-start(pred[256]{0:T(512)(128)(4,1)S(1)} %get-tuple-element.307) | copy-start | bytes 772
  17.7 11.4 %collective-permute-start.1 = (bf16[2,208,512]{2,1,0:T(8,128)(2,1)S(1)}, bf16[2,208,512]{2,1,0:T(8,128)(2,1)S(1)}, u32[]{:S(2)}, u32[]{:S(2)}) collective-permute-start(bf16[2,208,512]{2,1,0:T(8,128)(2,1)S(1)} %pad_maximum_fusion.11), channel_id=1, source_target_pairs={{0,8},{1,9},{2,10},{3,11},{4,12},{5,13},{6,14},{7,15},{8,0},{9,1},... | collective-permute-start | bytes 1277960 | tf_op jit(solution)/shard_map/ppermute | solution.py:1203
  19.8 13.8 %copy-start.37 = (s32[1,16]{1,0:T(1,128)S(1)}, s32[1,16]{1,0:T(1,128)}, u32[]{:S(2)}) copy-start(s32[1,16]{1,0:T(1,128)} %param.18) | copy-start | bytes 196
  29.3 14.5 %collective-permute-start.4 = (bf16[256,512]{1,0:T(8,128)(2,1)S(1)}, bf16[256,512]{1,0:T(8,128)(2,1)S(1)}, u32[]{:S(2)}, u32[]{:S(2)}) collective-permute-start(bf16[256,512]{1,0:T(8,128)(2,1)S(1)} %bitcast_select_fusion), channel_id=1, source_target_pairs={{0,16},{1,17},{2,18},{3,19},{4,20},{5,21},{6,22},{7,23},{8,24},{9,... | collective-permute-start | bytes 786440 | tf_op jit(solution)/shard_map/ppermute | solution.py:1203
  32.1 11.7 %collective-permute-start.2 = (bf16[2,208,512]{2,1,0:T(8,128)(2,1)S(1)}, bf16[2,208,512]{2,1,0:T(8,128)(2,1)S(1)}, u32[]{:S(2)}, u32[]{:S(2)}) collective-permute-start(bf16[2,208,512]{2,1,0:T(8,128)(2,1)S(1)} %get-tuple-element.121), channel_id=1, source_target_pairs={{0,2},{1,3},{2,0},{3,1},{4,6},{5,7},{6,4},{7,5},{8,10},{9,11},{10,... | collective-permute-start | bytes 1277960 | tf_op jit(solution)/shard_map/ppermute | solution.py:1203
  34.4 10.7 %collective-permute-start.3 = (bf16[2,208,512]{2,1,0:T(8,128)(2,1)S(1)}, bf16[2,208,512]{2,1,0:T(8,128)(2,1)S(1)}, u32[]{:S(2)}, u32[]{:S(2)}) collective-permute-start(bf16[2,208,512]{2,1,0:T(8,128)(2,1)S(1)} %get-tuple-element.122), channel_id=1, source_target_pairs={{0,4},{1,5},{2,6},{3,7},{4,0},{5,1},{6,2},{7,3},{8,12},{9,13},{10,... | collective-permute-start | bytes 1277960 | tf_op jit(solution)/shard_map/ppermute | solution.py:1203
  45.2 11.9 %collective-permute-start.7 = (bf16[2,256,512]{2,1,0:T(8,128)(2,1)S(1)}, bf16[2,256,512]{2,1,0:T(8,128)(2,1)S(1)}, u32[]{:S(2)}, u32[]{:S(2)}) collective-permute-start(bf16[2,256,512]{2,1,0:T(8,128)(2,1)S(1)} %pad_maximum_fusion.9), channel_id=1, source_target_pairs={{0,8},{1,9},{2,10},{3,11},{4,12},{5,13},{6,14},{7,15},{8,0},{9,1},... | collective-permute-start | bytes 1572872 | tf_op jit(solution)/shard_map/ppermute | solution.py:1203
  47.4 18.8 %collective-permute-start.5 = (bf16[2,2,208,512]{3,2,0,1:T(8,128)(2,1)S(1)}, bf16[2,2,208,512]{3,2,0,1:T(8,128)(2,1)S(1)}, u32[]{:S(2)}, u32[]{:S(2)}) collective-permute-start(bf16[2,2,208,512]{3,2,0,1:T(8,128)(2,1)S(1)} %pad_maximum_fusion.6), channel_id=1, source_target_pairs={{0,4},{1,5},{2,6},{3,7},{4,0},{5,1},{6,2},{7,3},{8,12},{9,13},{10,... | collective-permute-start | bytes 2555912 | tf_op jit(solution)/shard_map/ppermute | solution.py:1203
  49.4 18.5 %collective-permute-start.6 = (bf16[2,2,208,512]{3,2,0,1:T(8,128)(2,1)S(1)}, bf16[2,2,208,512]{3,2,0,1:T(8,128)(2,1)S(1)}, u32[]{:S(2)}, u32[]{:S(2)}) collective-permute-start(bf16[2,2,208,512]{3,2,0,1:T(8,128)(2,1)S(1)} %pad_maximum_fusion.7), channel_id=1, source_target_pairs={{0,2},{1,3},{2,0},{3,1},{4,6},{5,7},{6,4},{7,5},{8,10},{9,11},{10,... | collective-permute-start | bytes 2555912 | tf_op jit(solution)/shard_map/ppermute | solution.py:1203
  66.7 21.8 %copy-start.12 = (bf16[2,2,2,208,512]{4,3,2,1,0:T(8,128)(2,1)}, bf16[2,2,2,208,512]{4,3,2,1,0:T(8,128)(2,1)S(1)}, u32[]{:S(2)}) copy-start(bf16[2,2,2,208,512]{4,3,2,1,0:T(8,128)(2,1)S(1)} %copy.93) | copy-start | bytes 5111812
  68.3 20.2 %copy-start.22 = (bf16[2,2,2,208,512]{4,3,2,1,0:T(8,128)(2,1)}, bf16[2,2,2,208,512]{4,3,2,1,0:T(8,128)(2,1)S(1)}, u32[]{:S(2)}) copy-start(bf16[2,2,2,208,512]{4,3,2,1,0:T(8,128)(2,1)S(1)} %copy.94) | copy-start | bytes 5111812
  68.3 11.2 %collective-permute-start.8 = (bf16[2,256,512]{2,1,0:T(8,128)(2,1)S(1)}, bf16[2,256,512]{2,1,0:T(8,128)(2,1)S(1)}, u32[]{:S(2)}, u32[]{:S(2)}) collective-permute-start(bf16[2,256,512]{2,1,0:T(8,128)(2,1)S(1)} %get-tuple-element.129), channel_id=1, source_target_pairs={{0,2},{1,3},{2,0},{3,1},{4,6},{5,7},{6,4},{7,5},{8,10},{9,11},{10,... | collective-permute-start | bytes 1572872 | tf_op jit(solution)/shard_map/ppermute | solution.py:1203
  69.9 11.1 %collective-permute-start.9 = (bf16[2,256,512]{2,1,0:T(8,128)(2,1)S(1)}, bf16[2,256,512]{2,1,0:T(8,128)(2,1)S(1)}, u32[]{:S(2)}, u32[]{:S(2)}) collective-permute-start(bf16[2,256,512]{2,1,0:T(8,128)(2,1)S(1)} %get-tuple-element.130), channel_id=1, source_target_pairs={{0,4},{1,5},{2,6},{3,7},{4,0},{5,1},{6,2},{7,3},{8,12},{9,13},{10,... | collective-permute-start | bytes 1572872 | tf_op jit(solution)/shard_map/ppermute | solution.py:1203
  79.8 2.7 copy-start.26
  81.2 6.1 %collective-permute-start.10 = (bf16[8,208,512]{2,1,0:T(8,128)(2,1)S(1)}, bf16[8,208,512]{2,1,0:T(8,128)(2,1)S(1)}, u32[]{:S(2)}, u32[]{:S(2)}) collective-permute-start(bf16[8,208,512]{2,1,0:T(8,128)(2,1)S(1)} %bitcast.291), channel_id=1, source_target_pairs={{0,1},{1,0},{2,3},{3,2},{4,5},{5,4},{6,7},{7,6},{8,9},{9,8},{10,11... | collective-permute-start | bytes 5111816 | tf_op jit(solution)/shard_map/ppermute | solution.py:1203
  81.3 6.0 %collective-permute-start.11 = (bf16[8,208,512]{2,1,0:T(8,128)(2,1)S(1)}, bf16[8,208,512]{2,1,0:T(8,128)(2,1)S(1)}, u32[]{:S(2)}, u32[]{:S(2)}) collective-permute-start(bf16[8,208,512]{2,1,0:T(8,128)(2,1)S(1)} %bitcast.301), channel_id=1, source_target_pairs={{0,1},{1,0},{2,3},{3,2},{4,5},{5,4},{6,7},{7,6},{8,9},{9,8},{10,11... | collective-permute-start | bytes 5111816 | tf_op jit(solution)/shard_map/ppermute | solution.py:1203
  87.3 1.9 copy-start.21
  87.3 1.9 copy-start.27
  87.3 26.3 %collective-permute-start.12 = (bf16[2,2,256,512]{3,2,0,1:T(8,128)(2,1)S(1)}, bf16[2,2,256,512]{3,2,0,1:T(8,128)(2,1)S(1)}, u32[]{:S(2)}, u32[]{:S(2)}) collective-permute-start(bf16[2,2,256,512]{3,2,0,1:T(8,128)(2,1)S(1)} %pad_maximum_fusion.4), channel_id=1, source_target_pairs={{0,4},{1,5},{2,6},{3,7},{4,0},{5,1},{6,2},{7,3},{8,12},{9,13},{10,... | collective-permute-start | bytes 3145736 | tf_op jit(solution)/shard_map/ppermute | solution.py:1203
  88.0 26.1 %collective-permute-start.13 = (bf16[2,2,256,512]{3,2,0,1:T(8,128)(2,1)S(1)}, bf16[2,2,256,512]{3,2,0,1:T(8,128)(2,1)S(1)}, u32[]{:S(2)}, u32[]{:S(2)}) collective-permute-start(bf16[2,2,256,512]{3,2,0,1:T(8,128)(2,1)S(1)} %pad_maximum_fusion.5), channel_id=1, source_target_pairs={{0,2},{1,3},{2,0},{3,1},{4,6},{5,7},{6,4},{7,5},{8,10},{9,11},{10,... | collective-permute-start | bytes 3145736 | tf_op jit(solution)/shard_map/ppermute | solution.py:1203
  114.5 2.6 copy-start.23
  114.6 25.7 %copy-start.20 = (bf16[2,2,2,256,512]{4,3,2,1,0:T(8,128)(2,1)}, bf16[2,2,2,256,512]{4,3,2,1,0:T(8,128)(2,1)S(1)}, u32[]{:S(2)}) copy-start(bf16[2,2,2,256,512]{4,3,2,1,0:T(8,128)(2,1)S(1)} %copy.98) | copy-start | bytes 6291460
  115.4 4.6 %collective-permute-start.14 = (bf16[8,256,512]{2,1,0:T(8,128)(2,1)S(1)}, bf16[8,256,512]{2,1,0:T(8,128)(2,1)S(1)}, u32[]{:S(2)}, u32[]{:S(2)}) collective-permute-start(bf16[8,256,512]{2,1,0:T(8,128)(2,1)S(1)} %bitcast.284), channel_id=1, source_target_pairs={{0,1},{1,0},{2,3},{3,2},{4,5},{5,4},{6,7},{7,6},{8,9},{9,8},{10,11... | collective-permute-start | bytes 6291464 | tf_op jit(solution)/shard_map/ppermute | solution.py:1203
  116.3 24.0 %collective-permute-start.15 = (bf16[8,256,512]{2,1,0:T(8,128)(2,1)S(1)}, bf16[8,256,512]{2,1,0:T(8,128)(2,1)S(1)}, u32[]{:S(2)}, u32[]{:S(2)}) collective-permute-start(bf16[8,256,512]{2,1,0:T(8,128)(2,1)S(1)} %bitcast.299), channel_id=1, source_target_pairs={{0,1},{1,0},{2,3},{3,2},{4,5},{5,4},{6,7},{7,6},{8,9},{9,8},{10,11... | collective-permute-start | bytes 6291464 | tf_op jit(solution)/shard_map/ppermute | solution.py:1203
  212.2 23.3 %copy-start.2 = (bf16[32,4,16,512]{3,2,1,0:T(8,128)(2,1)S(1)}, bf16[32,4,16,512]{3,2,1,0:T(8,128)(2,1)}, u32[]{:S(2)}) copy-start(bf16[32,4,16,512]{3,2,1,0:T(8,128)(2,1)} %get-tuple-element.175) | copy-start | bytes 6291460
  212.2 23.3 %copy-start.3 = (bf16[2048,512]{1,0:T(8,128)(2,1)S(1)}, bf16[2048,512]{1,0:T(8,128)(2,1)}, u32[]{:S(2)}) copy-start(bf16[2048,512]{1,0:T(8,128)(2,1)} %get-tuple-element.176.refs_6_) | copy-start | bytes 6291460
  212.2 23.3 %copy-start.6 = (bf16[32,2,16,512]{3,2,1,0:T(8,128)(2,1)S(1)}, bf16[32,2,16,512]{3,2,1,0:T(8,128)(2,1)}, u32[]{:S(2)}) copy-start(bf16[32,2,16,512]{3,2,1,0:T(8,128)(2,1)} %get-tuple-element.173) | copy-start | bytes 3145732
  212.2 23.3 %copy-start.7 = (bf16[512,512]{1,0:T(8,128)(2,1)S(1)}, bf16[512,512]{1,0:T(8,128)(2,1)}, u32[]{:S(2)}) copy-start(bf16[512,512]{1,0:T(8,128)(2,1)} %get-tuple-element.174.refs_4_) | copy-start | bytes 1572868
  212.2 23.3 %copy-start.8 = (bf16[512,512]{1,0:T(8,128)(2,1)S(1)}, bf16[512,512]{1,0:T(8,128)(2,1)}, u32[]{:S(2)}) copy-start(bf16[512,512]{1,0:T(8,128)(2,1)} %get-tuple-element.172.refs_2_) | copy-start | bytes 1572868
  212.2 23.3 %copy-start.9 = (bf16[512,512]{1,0:T(8,128)(2,1)S(1)}, bf16[512,512]{1,0:T(8,128)(2,1)}, u32[]{:S(2)}) copy-start(bf16[512,512]{1,0:T(8,128)(2,1)} %get-tuple-element.171.refs_1_) | copy-start | bytes 1572868
  240.5 10.2 %collective-permute-start.16 = (bf16[16,256,512]{2,1,0:T(8,128)(2,1)}, bf16[16,256,512]{2,1,0:T(8,128)(2,1)}, u32[]{:S(2)}, u32[]{:S(2)}) collective-permute-start(bf16[16,256,512]{2,1,0:T(8,128)(2,1)} %get-tuple-element.182), channel_id=1, source_target_pairs={{0,1},{1,0},{2,3},{3,2},{4,5},{5,4},{6,7},{7,6},{8,9},{9,8},{10,11... | collective-permute-start | bytes 12582920 | tf_op jit(solution)/shard_map/ppermute | solution.py:1203
  242.0 8.7 %copy-start.14 = (bf16[16,256,512]{2,1,0:T(8,128)(2,1)S(1)}, bf16[16,256,512]{2,1,0:T(8,128)(2,1)}, u32[]{:S(2)}) copy-start(bf16[16,256,512]{2,1,0:T(8,128)(2,1)} %get-tuple-element.177) | copy-start | bytes 12582916
  258.0 35.0 %collective-permute-start.17 = (bf16[2,2,2,128,512]{4,3,1,0,2:T(8,128)(2,1)}, bf16[2,2,2,128,512]{4,3,1,0,2:T(8,128)(2,1)}, u32[]{:S(2)}, u32[]{:S(2)}) collective-permute-start(bf16[2,2,2,128,512]{4,3,1,0,2:T(8,128)(2,1)} %bitcast.273), channel_id=1, source_target_pairs={{0,4},{1,5},{2,6},{3,7},{4,0},{5,1},{6,2},{7,3},{8,12},{9,13},{10,... | collective-permute-start | bytes 3145736 | tf_op jit(solution)/shard_map/ppermute | solution.py:1203
  263.3 32.2 %collective-permute-start.18 = (bf16[2,2,2,128,512]{4,3,1,0,2:T(8,128)(2,1)}, bf16[2,2,2,128,512]{4,3,1,0,2:T(8,128)(2,1)}, u32[]{:S(2)}, u32[]{:S(2)}) collective-permute-start(bf16[2,2,2,128,512]{4,3,1,0,2:T(8,128)(2,1)} %bitcast.272), channel_id=1, source_target_pairs={{0,2},{1,3},{2,0},{3,1},{4,6},{5,7},{6,4},{7,5},{8,10},{9,11},{10,... | collective-permute-start | bytes 3145736 | tf_op jit(solution)/shard_map/ppermute | solution.py:1203
  294.6 2.4 copy-start.15
  297.9 20.2 %copy-start = (bf16[32,4,16,512]{3,2,1,0:T(8,128)(2,1)S(1)}, bf16[32,4,16,512]{3,2,1,0:T(8,128)(2,1)}, u32[]{:S(2)}) copy-start(bf16[32,4,16,512]{3,2,1,0:T(8,128)(2,1)} %get-tuple-element.204) | copy-start | bytes 6291460
  297.9 20.2 %copy-start.1 = (bf16[2048,512]{1,0:T(8,128)(2,1)S(1)}, bf16[2048,512]{1,0:T(8,128)(2,1)}, u32[]{:S(2)}) copy-start(bf16[2048,512]{1,0:T(8,128)(2,1)} %get-tuple-element.205.refs_3_) | copy-start | bytes 6291460
  297.9 20.2 %copy-start.10 = (bf16[512,512]{1,0:T(8,128)(2,1)S(1)}, bf16[512,512]{1,0:T(8,128)(2,1)}, u32[]{:S(2)}) copy-start(bf16[512,512]{1,0:T(8,128)(2,1)} %get-tuple-element.203.refs_1_) | copy-start | bytes 1572868
  322.9 11.8 %collective-permute-start.19 = (bf16[16,208,512]{2,1,0:T(8,128)(2,1)}, bf16[16,208,512]{2,1,0:T(8,128)(2,1)}, u32[]{:S(2)}, u32[]{:S(2)}) collective-permute-start(bf16[16,208,512]{2,1,0:T(8,128)(2,1)} %get-tuple-element.220), channel_id=1, source_target_pairs={{0,1},{1,0},{2,3},{3,2},{4,5},{5,4},{6,7},{7,6},{8,9},{9,8},{10,11... | collective-permute-start | bytes 10223624 | tf_op jit(solution)/shard_map/ppermute | solution.py:1203
  324.7 16.1 %collective-permute-start.24 = (bf16[2,2,128,512]{3,2,1,0:T(8,128)(2,1)}, bf16[2,2,128,512]{3,2,1,0:T(8,128)(2,1)S(1)}, u32[]{:S(2)}, u32[]{:S(2)}) collective-permute-start(bf16[2,2,128,512]{3,2,1,0:T(8,128)(2,1)} %dynamic-slice_bitcast_fusion.1), channel_id=1, source_target_pairs={{0,2},{1,3},{2,0},{3,1},{4,6},{5,7},{6,4},{7,5},{8,10},{9,11},{10,... | collective-permute-start | bytes 1572872 | tf_op jit(solution)/shard_map/ppermute | solution.py:1203
  326.6 14.4 %collective-permute-start.25 = (bf16[2,2,128,512]{3,2,1,0:T(8,128)(2,1)}, bf16[2,2,128,512]{3,2,1,0:T(8,128)(2,1)S(1)}, u32[]{:S(2)}, u32[]{:S(2)}) collective-permute-start(bf16[2,2,128,512]{3,2,1,0:T(8,128)(2,1)} %dynamic-slice_bitcast_fusion), channel_id=1, source_target_pairs={{0,4},{1,5},{2,6},{3,7},{4,0},{5,1},{6,2},{7,3},{8,12},{9,13},{10,... | collective-permute-start | bytes 1572872 | tf_op jit(solution)/shard_map/ppermute | solution.py:1203
  326.7 8.0 %copy-start.18 = (bf16[16,208,512]{2,1,0:T(8,128)(2,1)S(1)}, bf16[16,208,512]{2,1,0:T(8,128)(2,1)}, u32[]{:S(2)}) copy-start(bf16[16,208,512]{2,1,0:T(8,128)(2,1)} %get-tuple-element.219) | copy-start | bytes 10223620
  338.4 2.4 copy-start.16
  338.4 19.5 %collective-permute-start.22 = (bf16[2,2,2,96,512]{4,3,1,0,2:T(8,128)(2,1)S(1)}, bf16[2,2,2,96,512]{4,3,1,0,2:T(8,128)(2,1)S(1)}, u32[]{:S(2)}, u32[]{:S(2)}) collective-permute-start(bf16[2,2,2,96,512]{4,3,1,0,2:T(8,128)(2,1)S(1)} %bitcast.308), channel_id=1, source_target_pairs={{0,2},{1,3},{2,0},{3,1},{4,6},{5,7},{6,4},{7,5},{8,10},{9,11},{10,... | collective-permute-start | bytes 2359304 | tf_op jit(solution)/shard_map/ppermute | solution.py:1203
  340.5 23.4 %collective-permute-start.20 = (bf16[2,2,2,112,512]{4,3,1,0,2:T(8,128)(2,1)S(1)}, bf16[2,2,2,112,512]{4,3,1,0,2:T(8,128)(2,1)S(1)}, u32[]{:S(2)}, u32[]{:S(2)}) collective-permute-start(bf16[2,2,2,112,512]{4,3,1,0,2:T(8,128)(2,1)S(1)} %bitcast.307), channel_id=1, source_target_pairs={{0,4},{1,5},{2,6},{3,7},{4,0},{5,1},{6,2},{7,3},{8,12},{9,13},{10,... | collective-permute-start | bytes 2752520 | tf_op jit(solution)/shard_map/ppermute | solution.py:1203
  341.2 23.2 %collective-permute-start.26 = (bf16[256,512]{1,0:T(8,128)(2,1)S(1)}, bf16[256,512]{1,0:T(8,128)(2,1)S(1)}, u32[]{:S(2)}, u32[]{:S(2)}) collective-permute-start(bf16[256,512]{1,0:T(8,128)(2,1)S(1)} %get-tuple-element.263), channel_id=1, source_target_pairs={{0,8},{1,9},{2,10},{3,11},{4,12},{5,13},{6,14},{7,15},{8,0},{9,1},... | collective-permute-start | bytes 786440 | tf_op jit(solution)/shard_map/ppermute | solution.py:1203
  343.2 27.8 %collective-permute-start.27 = (bf16[256,512]{1,0:T(8,128)(2,1)S(1)}, bf16[256,512]{1,0:T(8,128)(2,1)S(1)}, u32[]{:S(2)}, u32[]{:S(2)}) collective-permute-start(bf16[256,512]{1,0:T(8,128)(2,1)S(1)} %get-tuple-element.264), channel_id=1, source_target_pairs={{0,16},{1,17},{2,18},{3,19},{4,20},{5,21},{6,22},{7,23},{8,24},{9,... | collective-permute-start | bytes 786440 | tf_op jit(solution)/shard_map/ppermute | solution.py:1203
  352.5 18.4 %collective-permute-start.28 = (bf16[256,512]{1,0:T(8,128)(2,1)S(1)}, bf16[256,512]{1,0:T(8,128)(2,1)S(1)}, u32[]{:S(2)}, u32[]{:S(2)}) collective-permute-start(bf16[256,512]{1,0:T(8,128)(2,1)S(1)} %get-tuple-element.265), channel_id=1, source_target_pairs={{0,24},{1,25},{2,26},{3,27},{4,28},{5,29},{6,30},{7,31},{8,16},{9,... | collective-permute-start | bytes 786440 | tf_op jit(solution)/shard_map/ppermute | solution.py:1203
  358.2 12.9 %collective-permute-start.23 = (bf16[2,2,96,512]{3,2,1,0:T(8,128)(2,1)S(1)}, bf16[2,2,96,512]{3,2,1,0:T(8,128)(2,1)S(1)}, u32[]{:S(2)}, u32[]{:S(2)}) collective-permute-start(bf16[2,2,96,512]{3,2,1,0:T(8,128)(2,1)S(1)} %dynamic-slice_bitcast_fusion.3), channel_id=1, source_target_pairs={{0,4},{1,5},{2,6},{3,7},{4,0},{5,1},{6,2},{7,3},{8,12},{9,13},{10,... | collective-permute-start | bytes 1179656 | tf_op jit(solution)/shard_map/ppermute | solution.py:1203
  364.2 9.1 %collective-permute-start.21 = (bf16[2,2,112,512]{3,2,1,0:T(8,128)(2,1)S(1)}, bf16[2,2,112,512]{3,2,1,0:T(8,128)(2,1)S(1)}, u32[]{:S(2)}, u32[]{:S(2)}) collective-permute-start(bf16[2,2,112,512]{3,2,1,0:T(8,128)(2,1)S(1)} %dynamic-slice_bitcast_fusion.2), channel_id=1, source_target_pairs={{0,2},{1,3},{2,0},{3,1},{4,6},{5,7},{6,4},{7,5},{8,10},{9,11},{10,... | collective-permute-start | bytes 1376264 | tf_op jit(solution)/shard_map/ppermute | solution.py:1203
  374.2 17.4 %collective-permute-start.29 = (bf16[208,512]{1,0:T(8,128)(2,1)}, bf16[208,512]{1,0:T(8,128)(2,1)S(1)}, u32[]{:S(2)}, u32[]{:S(2)}) collective-permute-start(bf16[208,512]{1,0:T(8,128)(2,1)} %get-tuple-element.223), channel_id=1, source_target_pairs={{0,8},{1,9},{2,10},{3,11},{4,12},{5,13},{6,14},{7,15},{8,0},{9,1},... | collective-permute-start | bytes 638984 | tf_op jit(solution)/shard_map/ppermute | solution.py:1203
  377.2 22.2 %collective-permute-start.30 = (bf16[208,512]{1,0:T(8,128)(2,1)}, bf16[208,512]{1,0:T(8,128)(2,1)}, u32[]{:S(2)}, u32[]{:S(2)}) collective-permute-start(bf16[208,512]{1,0:T(8,128)(2,1)} %get-tuple-element.224), channel_id=1, source_target_pairs={{0,16},{1,17},{2,18},{3,19},{4,20},{5,21},{6,22},{7,23},{8,24},{9,... | collective-permute-start | bytes 638984 | tf_op jit(solution)/shard_map/ppermute | solution.py:1203
  384.9 14.5 %collective-permute-start.31 = (bf16[208,512]{1,0:T(8,128)(2,1)}, bf16[208,512]{1,0:T(8,128)(2,1)}, u32[]{:S(2)}, u32[]{:S(2)}) collective-permute-start(bf16[208,512]{1,0:T(8,128)(2,1)} %get-tuple-element.225), channel_id=1, source_target_pairs={{0,24},{1,25},{2,26},{3,27},{4,28},{5,29},{6,30},{7,31},{8,16},{9,... | collective-permute-start | bytes 638984 | tf_op jit(solution)/shard_map/ppermute | solution.py:1203
  400.6 1.7 copy-start.24
  400.6 1.7 copy-start.25
  400.6 1.7 copy-start.31
  400.6 1.7 copy-start.33
  (7 other events, 9.1 us)
where the time goes:
time: 410 us; the launch traced here: 404 us
  Pallas kernels  207 us (50%)
  waiting for transfers between devices  80.4 us (20%)
  starting transfers between devices  57.4 us (14%)
  other arithmetic  33.1 us (8%)
  local copies, waits for them, and re-layouts  23.8 us (6%)
    pallas_call x11, Pallas kernels, run(): return made(plan, *placed)  207 us
    ppermute x32, waiting for transfers between devices, swap(): return lax.ppermute(values, 'fsdp', partner(bits))  80.4 us
    ppermute x32, starting transfers between devices, swap(): return lax.ppermute(values, 'fsdp', partner(bits))  57.4 us
    convert_element_type x10, other arithmetic, add_low(): return (former.astype(F32) + latter.astype(F32)).astype(LOW)  10.8 us
    unnamed x83, local copies, waits for them, and re-layouts  8.82 us
  transfers between devices with their start and end apart: 32, of which 15 were waited for; matrix products, arithmetic and copies ran while one was open for 8% of the time, Pallas kernels for 21%

commit v1 on v0

--- a/solution.py
+++ b/solution.py
@@ -446,6 +446,7 @@
         16 * number * width,
         name,
         room=44,
+        near=() if packed else (0,),
     )(plan, *([x, memory] if cross else [x]), *far[: sources_of(wanted)], small, owner, key_owner)
 
 

time: 410 us -> 411 us (level)
    ppermute x32, starting transfers between devices: 57.4 us -> 53.3 us  [swap(): return lax.ppermute(values, 'fsdp', partner(bits))]
    unnamed x83 -> x85, local copies, waits for them, and re-layouts: 8.82 us -> 8.83 us
  transfers between devices with their start and end apart: 32 -> 32, of which waited for: 15 -> 16; matrix products, arithmetic and copies ran while one was open for 8% -> 8% of each run, Pallas kernels for 21% -> 21%
where the time goes in v1:
time: 411 us; the launch traced here: 404 us
  Pallas kernels  209 us (51%)
  waiting for transfers between devices  83.7 us (20%)
  starting transfers between devices  53.3 us (13%)
  other arithmetic  32.1 us (8%)
  local copies, waits for them, and re-layouts  23.8 us (6%)
    pallas_call x11, Pallas kernels, run(): return made(plan, *placed)  209 us
    ppermute x32, waiting for transfers between devices, swap(): return lax.ppermute(values, 'fsdp', partner(bits))  83.7 us
    ppermute x32, starting transfers between devices, swap(): return lax.ppermute(values, 'fsdp', partner(bits))  53.3 us
    convert_element_type x10, other arithmetic, add_low(): return (former.astype(F32) + latter.astype(F32)).astype(LOW)  10.8 us
    unnamed x85, local copies, waits for them, and re-layouts  8.83 us
  transfers between devices with their start and end apart: 32, of which 16 were waited for; matrix products, arithmetic and copies ran while one was open for 8% of the time, Pallas kernels for 21%

profile of v1, /device:TPU:0, one launch (start us, length us, event | category | flops | bytes accessed | tf_op | source)
XLA Modules:
  0.0 404.5 jit_solution(16059994530388340035)
XLA Ops:
  0.7 1.1 convert_element_type.248
  3.4 4.1 %collective-permute-start = (bf16[208,512]{1,0:T(8,128)(2,1)S(1)}, bf16[208,512]{1,0:T(8,128)(2,1)S(1)}, u32[]{:S(2)}, u32[]{:S(2)}) collective-permute-start(bf16[208,512]{1,0:T(8,128)(2,1)S(1)} %pad_maximum_fusion.12), channel_id=1, source_target_pairs={{0,16},{1,17},{2,18},{3,19},{4,20},{5,21},{6,22},{7,23},{8,24},{9,... | collective-permute-start | bytes 638984 | tf_op jit(solution)/shard_map/ppermute | solution.py:1204
  8.1 9.4 %collective-permute-done = bf16[208,512]{1,0:T(8,128)(2,1)S(1)} collective-permute-done((bf16[208,512]{1,0:T(8,128)(2,1)S(1)}, bf16[208,512]{1,0:T(8,128)(2,1)S(1)}, u32[]{:S(2)}, u32[]{:S(2)}) %collective-permute-start) | collective-permute-done | bytes 213024 | tf_op jit(solution)/shard_map/ppermute | solution.py:1204
  20.0 9.1 %collective-permute-done.1 = bf16[2,208,512]{2,1,0:T(8,128)(2,1)S(1)} collective-permute-done((bf16[2,208,512]{2,1,0:T(8,128)(2,1)S(1)}, bf16[2,208,512]{2,1,0:T(8,128)(2,1)S(1)}, u32[]{:S(2)}, u32[]{:S(2)}) %collective-permute-start.1) | collective-permute-done | bytes 426016 | tf_op jit(solution)/shard_map/ppermute | solution.py:1204
  29.3 2.9 collective-permute-start.4
  32.1 1.5 collective-permute-start.2
  34.4 1.6 collective-permute-start.3
  36.0 7.8 %collective-permute-done.4 = bf16[256,512]{1,0:T(8,128)(2,1)S(1)} collective-permute-done((bf16[256,512]{1,0:T(8,128)(2,1)S(1)}, bf16[256,512]{1,0:T(8,128)(2,1)S(1)}, u32[]{:S(2)}, u32[]{:S(2)}) %collective-permute-start.4) | collective-permute-done | bytes 262176 | tf_op jit(solution)/shard_map/ppermute | solution.py:1204
  44.0 1.1 collective-permute-done.3
  45.2 1.5 collective-permute-start.7
  47.4 1.6 collective-permute-start.5
  50.0 7.2 %collective-permute-done.7 = bf16[2,256,512]{2,1,0:T(8,128)(2,1)S(1)} collective-permute-done((bf16[2,256,512]{2,1,0:T(8,128)(2,1)S(1)}, bf16[2,256,512]{2,1,0:T(8,128)(2,1)S(1)}, u32[]{:S(2)}, u32[]{:S(2)}) %collective-permute-start.7) | collective-permute-done | bytes 524320 | tf_op jit(solution)/shard_map/ppermute | solution.py:1204
  57.3 8.8 %collective-permute-done.5 = bf16[2,2,208,512]{3,2,0,1:T(8,128)(2,1)S(1)} collective-permute-done((bf16[2,2,208,512]{3,2,0,1:T(8,128)(2,1)S(1)}, bf16[2,2,208,512]{3,2,0,1:T(8,128)(2,1)S(1)}, u32[]{:S(2)}, u32[]{:S(2)}) %collective-permute-start.5) | collective-permute-done | bytes 852000 | tf_op jit(solution)/shard_map/ppermute | solution.py:1204
  66.7 1.2 collective-permute-done.6
  68.3 1.6 collective-permute-start.8
  71.1 8.5 %collective-permute-done.8 = bf16[2,256,512]{2,1,0:T(8,128)(2,1)S(1)} collective-permute-done((bf16[2,256,512]{2,1,0:T(8,128)(2,1)S(1)}, bf16[2,256,512]{2,1,0:T(8,128)(2,1)S(1)}, u32[]{:S(2)}, u32[]{:S(2)}) %collective-permute-start.8) | collective-permute-done | bytes 524320 | tf_op jit(solution)/shard_map/ppermute | solution.py:1204
  79.8 1.3 collective-permute-done.9
  85.4 1.9 fusion.35
  89.3 25.3 %enc_layer.1 = (bf16[1024,512]{1,0:T(8,128)(2,1)}, bf16[1024,1024]{1,0:T(8,128)(2,1)}, bf16[1024,512]{1,0:T(8,128)(2,1)}, f32[8,1024]{1,0:T(8,128)}, f32[1024,51...) custom-call(s32[3,8]{1,0:T(4,128)S(1)} %pad_add_fusion.2.plan, ...), custom_call_target="tpu_custom_call" | custom-call | flops 3221225472 | bytes 8388608 | tf_op jit(solution)/shard_map/enc_layer/pallas_call | solution.py:224
  116.4 1.8 collective-permute-start.14
  119.2 2.8 collective-permute-done.14.refs_2_.refs_4_.refs_13_.refs_6_
  122.0 1.4 copy-done.20
  123.3 18.4 %dec_block.1 = (bf16[1024,512]{1,0:T(8,128)(2,1)}, bf16[1024,1024]{1,0:T(8,128)(2,1)}, bf16[1024,512]{1,0:T(8,128)(2,1)}, f32[8,1024]{1,0:T(8,128)}, f32[1024,512]{1,0:T(8,128)}, /*index=5*/f32[1024,128]{1,0:T(8,128)}) custom-call(s32[3,8]{1,0:T(4,128)S(1)} %get-tuple-element.150.plan, bf16[1024,512]{1,0:T(8,128)(2,1)S(1)} %broadcast_select_fusion.refs_0_.refs_7_, ...), custom_call_target="tpu_custom_call" | custom-call | flops 3221225472 | bytes 8388608 | tf_op jit(solution)/shard_map/dec_block/pallas_call | solution.py:224
  141.8 1.3 copy-done.39
  143.1 41.8 %cross_turn.1 = (bf16[1024,512]{1,0:T(8,128)(2,1)}, bf16[1024,1024]{1,0:T(8,128)(2,1)}, f32[8,1024]{1,0:T(8,128)}, bf16[1024,512]{1,0:T(8,128)(2,1)}, f32[1024,5...) custom-call(s32[3,8]{1,0:T(4,128)} %get-tuple-element.149.plan, ...), custom_call_target="tpu_custom_call" | custom-call | flops 13958643712 | bytes 15728640 | tf_op jit(solution)/shard_map/cross_turn/pallas_call | solution.py:224
  184.9 28.6 %cross_back.1 = (f32[1024,512]{1,0:T(8,128)}, f32[1024,512]{1,0:T(8,128)}, bf16[1024,512]{1,0:T(8,128)(2,1)}, bf16[512,512]{1,0:T(8,128)(2,1)}, bf16[32,2,16,512...) custom-call(s32[3,8]{1,0:T(4,128)} %get-tuple-element.149.plan, ...), custom_call_target="tpu_custom_call" | custom-call | flops 6442450944 | bytes 12582912 | tf_op jit(solution)/shard_map/cross_back/pallas_call | solution.py:224
  213.6 23.2 %dec_back.1 = (bf16[1024,512]{1,0:T(8,128)(2,1)}, bf16[1024,512]{1,0:T(8,128)(2,1)}, bf16[1024,512]{1,0:T(8,128)(2,1)}, bf16[1536,512]{1,0:T(8,128)(2,1)}) custom-call(s32[3,8]{1,0:T(4,128)S(1)} %get-tuple-element.150.plan, bf16[1024,512]{1,0:T(8,128)(2,1)} %get-tuple-element.159.refs_0_, bf16[1024,1024]{1,0:T(8,128)(2,1)} %get-tuple-element.160.refs_1_.refs_2_, ...), custom_call_target="tpu_custom_call" | custom-call | flops 3758096384 | bytes 6291456 | tf_op jit(solution)/shard_map/dec_back/pallas_call | solution.py:224
  236.9 1.4 copy-done.4
  238.3 3.6 dec_pack.1
  241.9 2.9 collective-permute-start.16
  246.3 8.7 %dec_qkv_inputs.1 = (f32[1024,512]{1,0:T(8,128)}, f32[8,512]{1,0:T(8,128)}) custom-call(s32[3,8]{1,0:T(4,128)S(1)} %get-tuple-element.150.plan, bf16[1024,512]{1,0:T(8,128)(2,1)} %get-tuple-element.184.refs_0_, bf16[1024,512]{1,0:T(8,128)(2,1)} %get-tuple-element.185.refs_1_, bf16[1024,512]{1,0:T(8,128)(2,1)} %get-tuple-element.186.refs_2_, ...), custom_call_target="tpu_custom_call" | custom-call | flops 1610612736 | bytes 8388608 | tf_op jit(solution)/shard_map/dec_qkv_inputs/pallas_call | solution.py:224
  255.0 3.6 add_convert_fusion
  259.2 1.1 copy.139
  260.4 1.1 copy.140
  262.3 2.2 collective-permute-start.18
  264.4 26.5 %enc_ffn_back.1 = (f32[1024,512]{1,0:T(8,128)}, bf16[1024,512]{1,0:T(8,128)(2,1)}, bf16[32,4,16,512]{3,2,1,0:T(8,128)(2,1)}, bf16[2048,512]{1,0:T(8,128)(2,1)}, ...) custom-call(s32[3,8]{1,0:T(4,128)S(1)} %pad_add_fusion.2.plan, bf16[1024,512]{1,0:T(8,128)(2,1)} %refs_0_.2, ...), custom_call_target="tpu_custom_call" | custom-call | flops 10737418240 | bytes 15728640 | tf_op jit(solution)/shard_map/enc_ffn_back/pallas_call | solution.py:224
  292.0 0.9 pad.4.clone
  292.9 1.3 reshape.741.refs_4_
  294.2 1.5 fusion.1
  295.7 0.9 dynamic-slice_bitcast_fusion.1
  296.6 1.5 fusion
  299.0 21.8 %enc_back.1 = (bf16[1024,512]{1,0:T(8,128)(2,1)}, bf16[1024,512]{1,0:T(8,128)(2,1)}, bf16[1024,512]{1,0:T(8,128)(2,1)}, bf16[32,3,16,512]{3,2,1,0:T(8,128)(2,1)}) custom-call(s32[3,8]{1,0:T(4,128)S(1)} %pad_add_fusion.2.plan, bf16[1024,512]{1,0:T(8,128)(2,1)} %get-tuple-element.157.refs_0_, bf16[1024,1024]{1,0:T(8,128)(2,1)} %get-tuple-element.158.refs_1_.refs_2_, ...), custom_call_target="tpu_custom_call" | custom-call | flops 3758096384 | bytes 6291456 | tf_op jit(solution)/shard_map/enc_back/pallas_call | solution.py:224
  320.8 1.4 copy-done.5
  322.2 3.3 enc_pack.1
  325.6 3.0 collective-permute-start.19
  329.2 8.0 %enc_qkv_inputs.1 = f32[1024,512]{1,0:T(8,128)} custom-call(s32[3,8]{1,0:T(4,128)S(1)} %pad_add_fusion.2.plan, bf16[1024,512]{1,0:T(8,128)(2,1)} %get-tuple-element.214.refs_0_, bf16[1024,512]{1,0:T(8,128)(2,1)} %get-tuple-element.215.refs_1_, bf16[1024,512]{1,0:T(8,128)(2,1)} %get-tuple-element.216.refs_2_, f32[1024,512]{1,0:T(8,128)} %get-tuple-element.217.refs_3_, ...), custom_call_target="tpu_custom_call" | custom-call | flops 1610612736 | bytes 8388608 | tf_op jit(solution)/shard_map/enc_qkv_inputs/pallas_call | solution.py:224
  337.2 3.1 add_convert_fusion.1
  340.8 1.5 collective-permute-start.22
  342.6 2.1 collective-permute-start.20
  345.2 7.6 %collective-permute-start.27 = (bf16[256,512]{1,0:T(8,128)(2,1)S(1)}, bf16[256,512]{1,0:T(8,128)(2,1)S(1)}, u32[]{:S(2)}, u32[]{:S(2)}) collective-permute-start(bf16[256,512]{1,0:T(8,128)(2,1)S(1)} %get-tuple-element.264), channel_id=1, source_target_pairs={{0,16},{1,17},{2,18},{3,19},{4,20},{5,21},{6,22},{7,23},{8,24},{9,... | collective-permute-start | bytes 786440 | tf_op jit(solution)/shard_map/ppermute | solution.py:1204
  352.7 1.4 collective-permute-start.28
  354.1 6.1 %collective-permute-done.22 = bf16[2,2,2,96,512]{4,3,1,0,2:T(8,128)(2,1)S(1)} collective-permute-done((bf16[2,2,2,96,512]{4,3,1,0,2:T(8,128)(2,1)S(1)}, bf16[2,2,2,96,512]{4,3,1,0,2:T(8,128)(2,1)S(1)}, u32[]{:S(2)}, u32[]{:S(2)}) %collective-permute-start.22) | collective-permute-done | bytes 786464 | tf_op jit(solution)/shard_map/ppermute | solution.py:1204
  360.5 1.6 collective-permute-start.23
  362.1 3.9 collective-permute-done.20
  366.9 4.3 %collective-permute-done.27 = bf16[256,512]{1,0:T(8,128)(2,1)S(1)} collective-permute-done((bf16[256,512]{1,0:T(8,128)(2,1)S(1)}, bf16[256,512]{1,0:T(8,128)(2,1)S(1)}, u32[]{:S(2)}, u32[]{:S(2)}) %collective-permute-start.27) | collective-permute-done | bytes 262176 | tf_op jit(solution)/shard_map/ppermute | solution.py:1204
  371.3 1.5 collective-permute-done.23
  373.0 2.9 collective-permute-done.21
  377.4 7.7 %collective-permute-start.30 = (bf16[208,512]{1,0:T(8,128)(2,1)}, bf16[208,512]{1,0:T(8,128)(2,1)}, u32[]{:S(2)}, u32[]{:S(2)}) collective-permute-start(bf16[208,512]{1,0:T(8,128)(2,1)} %get-tuple-element.224), channel_id=1, source_target_pairs={{0,16},{1,17},{2,18},{3,19},{4,20},{5,21},{6,22},{7,23},{8,24},{9,... | collective-permute-start | bytes 638984 | tf_op jit(solution)/shard_map/ppermute | solution.py:1204
  385.1 1.5 collective-permute-start.31
  387.5 1.2 reshape.750
  388.7 3.1 fusion.48
  391.8 7.8 %collective-permute-done.30 = bf16[208,512]{1,0:T(8,128)(2,1)} collective-permute-done((bf16[208,512]{1,0:T(8,128)(2,1)}, bf16[208,512]{1,0:T(8,128)(2,1)}, u32[]{:S(2)}, u32[]{:S(2)}) %collective-permute-start.30) | collective-permute-done | bytes 213024 | tf_op jit(solution)/shard_map/ppermute | solution.py:1204
  399.6 1.1 fusion.17
  402.5 1.5 fusion.49
  (229 shorter events, 31.0 us)
Async XLA Ops:
  0.6 2.6 copy-start.18
  0.7 6.8 %copy-start.37 = (s32[1,16]{1,0:T(1,128)S(1)}, s32[1,16]{1,0:T(1,128)}, u32[]{:S(2)}) copy-start(s32[1,16]{1,0:T(1,128)} %param.19) | copy-start | bytes 196
  1.9 17.4 %copy-start.14 = (f32[256,512]{1,0:T(8,128)S(1)}, f32[256,512]{1,0:T(8,128)}, u32[]{:S(2)}) copy-start(f32[256,512]{1,0:T(8,128)} %param.26) | copy-start | bytes 1572868
  2.0 17.2 %copy-start.31 = (pred[192]{0:T(512)(128)(4,1)}, pred[192]{0:T(512)(128)(4,1)S(1)}, u32[]{:S(2)}) copy-start(pred[192]{0:T(512)(128)(4,1)S(1)} %get-tuple-element.304) | copy-start | bytes 580
  2.0 17.2 %copy-start.33 = (pred[192]{0:T(512)(128)(4,1)}, pred[192]{0:T(512)(128)(4,1)S(1)}, u32[]{:S(2)}) copy-start(pred[192]{0:T(512)(128)(4,1)S(1)} %get-tuple-element.305) | copy-start | bytes 580
  3.4 14.2 %collective-permute-start = (bf16[208,512]{1,0:T(8,128)(2,1)S(1)}, bf16[208,512]{1,0:T(8,128)(2,1)S(1)}, u32[]{:S(2)}, u32[]{:S(2)}) collective-permute-start(bf16[208,512]{1,0:T(8,128)(2,1)S(1)} %pad_maximum_fusion.12), channel_id=1, source_target_pairs={{0,16},{1,17},{2,18},{3,19},{4,20},{5,21},{6,22},{7,23},{8,24},{9,... | collective-permute-start | bytes 638984 | tf_op jit(solution)/shard_map/ppermute | solution.py:1204
  8.1 11.7 %copy-start.35 = (pred[256]{0:T(512)(128)(4,1)}, pred[256]{0:T(512)(128)(4,1)S(1)}, u32[]{:S(2)}) copy-start(pred[256]{0:T(512)(128)(4,1)S(1)} %get-tuple-element.306) | copy-start | bytes 772
  8.1 11.7 %copy-start.36 = (pred[256]{0:T(512)(128)(4,1)}, pred[256]{0:T(512)(128)(4,1)S(1)}, u32[]{:S(2)}) copy-start(pred[256]{0:T(512)(128)(4,1)S(1)} %get-tuple-element.307) | copy-start | bytes 772
  17.7 11.4 %collective-permute-start.1 = (bf16[2,208,512]{2,1,0:T(8,128)(2,1)S(1)}, bf16[2,208,512]{2,1,0:T(8,128)(2,1)S(1)}, u32[]{:S(2)}, u32[]{:S(2)}) collective-permute-start(bf16[2,208,512]{2,1,0:T(8,128)(2,1)S(1)} %pad_maximum_fusion.11), channel_id=1, source_target_pairs={{0,8},{1,9},{2,10},{3,11},{4,12},{5,13},{6,14},{7,15},{8,0},{9,1},... | collective-permute-start | bytes 1277960 | tf_op jit(solution)/shard_map/ppermute | solution.py:1204
  19.8 13.8 %copy-start.38 = (s32[1,16]{1,0:T(1,128)S(1)}, s32[1,16]{1,0:T(1,128)}, u32[]{:S(2)}) copy-start(s32[1,16]{1,0:T(1,128)} %param.18) | copy-start | bytes 196
  29.3 14.5 %collective-permute-start.4 = (bf16[256,512]{1,0:T(8,128)(2,1)S(1)}, bf16[256,512]{1,0:T(8,128)(2,1)S(1)}, u32[]{:S(2)}, u32[]{:S(2)}) collective-permute-start(bf16[256,512]{1,0:T(8,128)(2,1)S(1)} %bitcast_select_fusion), channel_id=1, source_target_pairs={{0,16},{1,17},{2,18},{3,19},{4,20},{5,21},{6,22},{7,23},{8,24},{9,... | collective-permute-start | bytes 786440 | tf_op jit(solution)/shard_map/ppermute | solution.py:1204
  32.1 11.7 %collective-permute-start.2 = (bf16[2,208,512]{2,1,0:T(8,128)(2,1)S(1)}, bf16[2,208,512]{2,1,0:T(8,128)(2,1)S(1)}, u32[]{:S(2)}, u32[]{:S(2)}) collective-permute-start(bf16[2,208,512]{2,1,0:T(8,128)(2,1)S(1)} %get-tuple-element.121), channel_id=1, source_target_pairs={{0,2},{1,3},{2,0},{3,1},{4,6},{5,7},{6,4},{7,5},{8,10},{9,11},{10,... | collective-permute-start | bytes 1277960 | tf_op jit(solution)/shard_map/ppermute | solution.py:1204
  34.4 10.7 %collective-permute-start.3 = (bf16[2,208,512]{2,1,0:T(8,128)(2,1)S(1)}, bf16[2,208,512]{2,1,0:T(8,128)(2,1)S(1)}, u32[]{:S(2)}, u32[]{:S(2)}) collective-permute-start(bf16[2,208,512]{2,1,0:T(8,128)(2,1)S(1)} %get-tuple-element.122), channel_id=1, source_target_pairs={{0,4},{1,5},{2,6},{3,7},{4,0},{5,1},{6,2},{7,3},{8,12},{9,13},{10,... | collective-permute-start | bytes 1277960 | tf_op jit(solution)/shard_map/ppermute | solution.py:1204
  45.2 11.9 %collective-permute-start.7 = (bf16[2,256,512]{2,1,0:T(8,128)(2,1)S(1)}, bf16[2,256,512]{2,1,0:T(8,128)(2,1)S(1)}, u32[]{:S(2)}, u32[]{:S(2)}) collective-permute-start(bf16[2,256,512]{2,1,0:T(8,128)(2,1)S(1)} %pad_maximum_fusion.9), channel_id=1, source_target_pairs={{0,8},{1,9},{2,10},{3,11},{4,12},{5,13},{6,14},{7,15},{8,0},{9,1},... | collective-permute-start | bytes 1572872 | tf_op jit(solution)/shard_map/ppermute | solution.py:1204
  47.4 18.8 %collective-permute-start.5 = (bf16[2,2,208,512]{3,2,0,1:T(8,128)(2,1)S(1)}, bf16[2,2,208,512]{3,2,0,1:T(8,128)(2,1)S(1)}, u32[]{:S(2)}, u32[]{:S(2)}) collective-permute-start(bf16[2,2,208,512]{3,2,0,1:T(8,128)(2,1)S(1)} %pad_maximum_fusion.6), channel_id=1, source_target_pairs={{0,4},{1,5},{2,6},{3,7},{4,0},{5,1},{6,2},{7,3},{8,12},{9,13},{10,... | collective-permute-start | bytes 2555912 | tf_op jit(solution)/shard_map/ppermute | solution.py:1204
  49.4 18.5 %collective-permute-start.6 = (bf16[2,2,208,512]{3,2,0,1:T(8,128)(2,1)S(1)}, bf16[2,2,208,512]{3,2,0,1:T(8,128)(2,1)S(1)}, u32[]{:S(2)}, u32[]{:S(2)}) collective-permute-start(bf16[2,2,208,512]{3,2,0,1:T(8,128)(2,1)S(1)} %pad_maximum_fusion.7), channel_id=1, source_target_pairs={{0,2},{1,3},{2,0},{3,1},{4,6},{5,7},{6,4},{7,5},{8,10},{9,11},{10,... | collective-permute-start | bytes 2555912 | tf_op jit(solution)/shard_map/ppermute | solution.py:1204
  66.7 21.8 %copy-start.13 = (bf16[2,2,2,208,512]{4,3,2,1,0:T(8,128)(2,1)}, bf16[2,2,2,208,512]{4,3,2,1,0:T(8,128)(2,1)S(1)}, u32[]{:S(2)}) copy-start(bf16[2,2,2,208,512]{4,3,2,1,0:T(8,128)(2,1)S(1)} %copy.93) | copy-start | bytes 5111812
  68.3 20.2 %copy-start.23 = (bf16[2,2,2,208,512]{4,3,2,1,0:T(8,128)(2,1)}, bf16[2,2,2,208,512]{4,3,2,1,0:T(8,128)(2,1)S(1)}, u32[]{:S(2)}) copy-start(bf16[2,2,2,208,512]{4,3,2,1,0:T(8,128)(2,1)S(1)} %copy.94) | copy-start | bytes 5111812
  68.3 11.2 %collective-permute-start.8 = (bf16[2,256,512]{2,1,0:T(8,128)(2,1)S(1)}, bf16[2,256,512]{2,1,0:T(8,128)(2,1)S(1)}, u32[]{:S(2)}, u32[]{:S(2)}) collective-permute-start(bf16[2,256,512]{2,1,0:T(8,128)(2,1)S(1)} %get-tuple-element.129), channel_id=1, source_target_pairs={{0,2},{1,3},{2,0},{3,1},{4,6},{5,7},{6,4},{7,5},{8,10},{9,11},{10,... | collective-permute-start | bytes 1572872 | tf_op jit(solution)/shard_map/ppermute | solution.py:1204
  69.9 11.1 %collective-permute-start.9 = (bf16[2,256,512]{2,1,0:T(8,128)(2,1)S(1)}, bf16[2,256,512]{2,1,0:T(8,128)(2,1)S(1)}, u32[]{:S(2)}, u32[]{:S(2)}) collective-permute-start(bf16[2,256,512]{2,1,0:T(8,128)(2,1)S(1)} %get-tuple-element.130), channel_id=1, source_target_pairs={{0,4},{1,5},{2,6},{3,7},{4,0},{5,1},{6,2},{7,3},{8,12},{9,13},{10,... | collective-permute-start | bytes 1572872 | tf_op jit(solution)/shard_map/ppermute | solution.py:1204
  79.8 2.7 copy-start.27
  81.2 6.1 %collective-permute-start.10 = (bf16[8,208,512]{2,1,0:T(8,128)(2,1)S(1)}, bf16[8,208,512]{2,1,0:T(8,128)(2,1)S(1)}, u32[]{:S(2)}, u32[]{:S(2)}) collective-permute-start(bf16[8,208,512]{2,1,0:T(8,128)(2,1)S(1)} %bitcast.291), channel_id=1, source_target_pairs={{0,1},{1,0},{2,3},{3,2},{4,5},{5,4},{6,7},{7,6},{8,9},{9,8},{10,11... | collective-permute-start | bytes 5111816 | tf_op jit(solution)/shard_map/ppermute | solution.py:1204
  81.3 6.0 %collective-permute-start.11 = (bf16[8,208,512]{2,1,0:T(8,128)(2,1)S(1)}, bf16[8,208,512]{2,1,0:T(8,128)(2,1)S(1)}, u32[]{:S(2)}, u32[]{:S(2)}) collective-permute-start(bf16[8,208,512]{2,1,0:T(8,128)(2,1)S(1)} %bitcast.301), channel_id=1, source_target_pairs={{0,1},{1,0},{2,3},{3,2},{4,5},{5,4},{6,7},{7,6},{8,9},{9,8},{10,11... | collective-permute-start | bytes 5111816 | tf_op jit(solution)/shard_map/ppermute | solution.py:1204
  87.3 1.9 copy-start.22
  87.3 1.9 copy-start.28
  87.3 27.2 %collective-permute-start.12 = (bf16[2,2,256,512]{3,2,0,1:T(8,128)(2,1)S(1)}, bf16[2,2,256,512]{3,2,0,1:T(8,128)(2,1)S(1)}, u32[]{:S(2)}, u32[]{:S(2)}) collective-permute-start(bf16[2,2,256,512]{3,2,0,1:T(8,128)(2,1)S(1)} %pad_maximum_fusion.4), channel_id=1, source_target_pairs={{0,4},{1,5},{2,6},{3,7},{4,0},{5,1},{6,2},{7,3},{8,12},{9,13},{10,... | collective-permute-start | bytes 3145736 | tf_op jit(solution)/shard_map/ppermute | solution.py:1204
  88.0 27.1 %collective-permute-start.13 = (bf16[2,2,256,512]{3,2,0,1:T(8,128)(2,1)S(1)}, bf16[2,2,256,512]{3,2,0,1:T(8,128)(2,1)S(1)}, u32[]{:S(2)}, u32[]{:S(2)}) collective-permute-start(bf16[2,2,256,512]{3,2,0,1:T(8,128)(2,1)S(1)} %pad_maximum_fusion.5), channel_id=1, source_target_pairs={{0,2},{1,3},{2,0},{3,1},{4,6},{5,7},{6,4},{7,5},{8,10},{9,11},{10,... | collective-permute-start | bytes 3145736 | tf_op jit(solution)/shard_map/ppermute | solution.py:1204
  115.4 3.5 copy-start.24
  115.6 26.1 %copy-start.21 = (bf16[2,2,2,256,512]{4,3,2,1,0:T(8,128)(2,1)}, bf16[2,2,2,256,512]{4,3,2,1,0:T(8,128)(2,1)S(1)}, u32[]{:S(2)}) copy-start(bf16[2,2,2,256,512]{4,3,2,1,0:T(8,128)(2,1)S(1)} %copy.98) | copy-start | bytes 6291460
  116.4 5.6 %collective-permute-start.14 = (bf16[8,256,512]{2,1,0:T(8,128)(2,1)S(1)}, bf16[8,256,512]{2,1,0:T(8,128)(2,1)S(1)}, u32[]{:S(2)}, u32[]{:S(2)}) collective-permute-start(bf16[8,256,512]{2,1,0:T(8,128)(2,1)S(1)} %bitcast.284), channel_id=1, source_target_pairs={{0,1},{1,0},{2,3},{3,2},{4,5},{5,4},{6,7},{7,6},{8,9},{9,8},{10,11... | collective-permute-start | bytes 6291464 | tf_op jit(solution)/shard_map/ppermute | solution.py:1204
  118.2 23.6 %collective-permute-start.15 = (bf16[8,256,512]{2,1,0:T(8,128)(2,1)S(1)}, bf16[8,256,512]{2,1,0:T(8,128)(2,1)S(1)}, u32[]{:S(2)}, u32[]{:S(2)}) collective-permute-start(bf16[8,256,512]{2,1,0:T(8,128)(2,1)S(1)} %bitcast.299), channel_id=1, source_target_pairs={{0,1},{1,0},{2,3},{3,2},{4,5},{5,4},{6,7},{7,6},{8,9},{9,8},{10,11... | collective-permute-start | bytes 6291464 | tf_op jit(solution)/shard_map/ppermute | solution.py:1204
  119.2 22.6 %copy-start.7 = (bf16[1024,512]{1,0:T(8,128)(2,1)}, bf16[1024,512]{1,0:T(8,128)(2,1)S(1)}, u32[]{:S(2)}) copy-start(bf16[1024,512]{1,0:T(8,128)(2,1)S(1)} %broadcast_select_fusion.refs_0_.refs_7_) | copy-start | bytes 3145732
  213.6 23.3 %copy-start.2 = (bf16[32,4,16,512]{3,2,1,0:T(8,128)(2,1)S(1)}, bf16[32,4,16,512]{3,2,1,0:T(8,128)(2,1)}, u32[]{:S(2)}) copy-start(bf16[32,4,16,512]{3,2,1,0:T(8,128)(2,1)} %get-tuple-element.175) | copy-start | bytes 6291460
  213.6 23.3 %copy-start.3 = (bf16[2048,512]{1,0:T(8,128)(2,1)S(1)}, bf16[2048,512]{1,0:T(8,128)(2,1)}, u32[]{:S(2)}) copy-start(bf16[2048,512]{1,0:T(8,128)(2,1)} %get-tuple-element.176.refs_6_) | copy-start | bytes 6291460
  213.6 23.3 %copy-start.6 = (bf16[32,2,16,512]{3,2,1,0:T(8,128)(2,1)S(1)}, bf16[32,2,16,512]{3,2,1,0:T(8,128)(2,1)}, u32[]{:S(2)}) copy-start(bf16[32,2,16,512]{3,2,1,0:T(8,128)(2,1)} %get-tuple-element.173) | copy-start | bytes 3145732
  213.6 23.3 %copy-start.8 = (bf16[512,512]{1,0:T(8,128)(2,1)S(1)}, bf16[512,512]{1,0:T(8,128)(2,1)}, u32[]{:S(2)}) copy-start(bf16[512,512]{1,0:T(8,128)(2,1)} %get-tuple-element.174.refs_4_) | copy-start | bytes 1572868
  213.6 23.3 %copy-start.9 = (bf16[512,512]{1,0:T(8,128)(2,1)S(1)}, bf16[512,512]{1,0:T(8,128)(2,1)}, u32[]{:S(2)}) copy-start(bf16[512,512]{1,0:T(8,128)(2,1)} %get-tuple-element.172.refs_2_) | copy-start | bytes 1572868
  213.6 23.3 %copy-start.10 = (bf16[512,512]{1,0:T(8,128)(2,1)S(1)}, bf16[512,512]{1,0:T(8,128)(2,1)}, u32[]{:S(2)}) copy-start(bf16[512,512]{1,0:T(8,128)(2,1)} %get-tuple-element.171.refs_1_) | copy-start | bytes 1572868
  241.9 13.0 %collective-permute-start.16 = (bf16[16,256,512]{2,1,0:T(8,128)(2,1)}, bf16[16,256,512]{2,1,0:T(8,128)(2,1)}, u32[]{:S(2)}, u32[]{:S(2)}) collective-permute-start(bf16[16,256,512]{2,1,0:T(8,128)(2,1)} %get-tuple-element.182), channel_id=1, source_target_pairs={{0,1},{1,0},{2,3},{3,2},{4,5},{5,4},{6,7},{7,6},{8,9},{9,8},{10,11... | collective-permute-start | bytes 12582920 | tf_op jit(solution)/shard_map/ppermute | solution.py:1204
  246.3 8.7 %copy-start.15 = (bf16[16,256,512]{2,1,0:T(8,128)(2,1)S(1)}, bf16[16,256,512]{2,1,0:T(8,128)(2,1)}, u32[]{:S(2)}) copy-start(bf16[16,256,512]{2,1,0:T(8,128)(2,1)} %get-tuple-element.177) | copy-start | bytes 12582916
  262.3 31.9 %collective-permute-start.17 = (bf16[2,2,2,128,512]{4,3,1,0,2:T(8,128)(2,1)}, bf16[2,2,2,128,512]{4,3,1,0,2:T(8,128)(2,1)}, u32[]{:S(2)}, u32[]{:S(2)}) collective-permute-start(bf16[2,2,2,128,512]{4,3,1,0,2:T(8,128)(2,1)} %bitcast.273), channel_id=1, source_target_pairs={{0,4},{1,5},{2,6},{3,7},{4,0},{5,1},{6,2},{7,3},{8,12},{9,13},{10,... | collective-permute-start | bytes 3145736 | tf_op jit(solution)/shard_map/ppermute | solution.py:1204
  262.3 34.4 %collective-permute-start.18 = (bf16[2,2,2,128,512]{4,3,1,0,2:T(8,128)(2,1)}, bf16[2,2,2,128,512]{4,3,1,0,2:T(8,128)(2,1)}, u32[]{:S(2)}, u32[]{:S(2)}) collective-permute-start(bf16[2,2,2,128,512]{4,3,1,0,2:T(8,128)(2,1)} %bitcast.272), channel_id=1, source_target_pairs={{0,2},{1,3},{2,0},{3,1},{4,6},{5,7},{6,4},{7,5},{8,10},{9,11},{10,... | collective-permute-start | bytes 3145736 | tf_op jit(solution)/shard_map/ppermute | solution.py:1204
  295.7 2.5 copy-start.16
  299.0 21.8 %copy-start = (bf16[32,4,16,512]{3,2,1,0:T(8,128)(2,1)S(1)}, bf16[32,4,16,512]{3,2,1,0:T(8,128)(2,1)}, u32[]{:S(2)}) copy-start(bf16[32,4,16,512]{3,2,1,0:T(8,128)(2,1)} %get-tuple-element.204) | copy-start | bytes 6291460
  299.0 21.8 %copy-start.1 = (bf16[2048,512]{1,0:T(8,128)(2,1)S(1)}, bf16[2048,512]{1,0:T(8,128)(2,1)}, u32[]{:S(2)}) copy-start(bf16[2048,512]{1,0:T(8,128)(2,1)} %get-tuple-element.205.refs_3_) | copy-start | bytes 6291460
  299.0 21.8 %copy-start.11 = (bf16[512,512]{1,0:T(8,128)(2,1)S(1)}, bf16[512,512]{1,0:T(8,128)(2,1)}, u32[]{:S(2)}) copy-start(bf16[512,512]{1,0:T(8,128)(2,1)} %get-tuple-element.203.refs_1_) | copy-start | bytes 1572868
  325.6 11.6 %collective-permute-start.19 = (bf16[16,208,512]{2,1,0:T(8,128)(2,1)}, bf16[16,208,512]{2,1,0:T(8,128)(2,1)}, u32[]{:S(2)}, u32[]{:S(2)}) collective-permute-start(bf16[16,208,512]{2,1,0:T(8,128)(2,1)} %get-tuple-element.220), channel_id=1, source_target_pairs={{0,1},{1,0},{2,3},{3,2},{4,5},{5,4},{6,7},{7,6},{8,9},{9,8},{10,11... | collective-permute-start | bytes 10223624 | tf_op jit(solution)/shard_map/ppermute | solution.py:1204
  328.6 16.1 %collective-permute-start.24 = (bf16[2,2,128,512]{3,2,1,0:T(8,128)(2,1)}, bf16[2,2,128,512]{3,2,1,0:T(8,128)(2,1)S(1)}, u32[]{:S(2)}, u32[]{:S(2)}) collective-permute-start(bf16[2,2,128,512]{3,2,1,0:T(8,128)(2,1)} %dynamic-slice_bitcast_fusion.1), channel_id=1, source_target_pairs={{0,2},{1,3},{2,0},{3,1},{4,6},{5,7},{6,4},{7,5},{8,10},{9,11},{10,... | collective-permute-start | bytes 1572872 | tf_op jit(solution)/shard_map/ppermute | solution.py:1204
  328.6 16.2 %collective-permute-start.25 = (bf16[2,2,128,512]{3,2,1,0:T(8,128)(2,1)}, bf16[2,2,128,512]{3,2,1,0:T(8,128)(2,1)S(1)}, u32[]{:S(2)}, u32[]{:S(2)}) collective-permute-start(bf16[2,2,128,512]{3,2,1,0:T(8,128)(2,1)} %dynamic-slice_bitcast_fusion), channel_id=1, source_target_pairs={{0,4},{1,5},{2,6},{3,7},{4,0},{5,1},{6,2},{7,3},{8,12},{9,13},{10,... | collective-permute-start | bytes 1572872 | tf_op jit(solution)/shard_map/ppermute | solution.py:1204
  329.2 8.0 %copy-start.19 = (bf16[16,208,512]{2,1,0:T(8,128)(2,1)S(1)}, bf16[16,208,512]{2,1,0:T(8,128)(2,1)}, u32[]{:S(2)}) copy-start(bf16[16,208,512]{2,1,0:T(8,128)(2,1)} %get-tuple-element.219) | copy-start | bytes 10223620
  340.8 3.9 copy-start.17
  340.8 19.4 %collective-permute-start.22 = (bf16[2,2,2,96,512]{4,3,1,0,2:T(8,128)(2,1)S(1)}, bf16[2,2,2,96,512]{4,3,1,0,2:T(8,128)(2,1)S(1)}, u32[]{:S(2)}, u32[]{:S(2)}) collective-permute-start(bf16[2,2,2,96,512]{4,3,1,0,2:T(8,128)(2,1)S(1)} %bitcast.308), channel_id=1, source_target_pairs={{0,2},{1,3},{2,0},{3,1},{4,6},{5,7},{6,4},{7,5},{8,10},{9,11},{10,... | collective-permute-start | bytes 2359304 | tf_op jit(solution)/shard_map/ppermute | solution.py:1204
  342.6 23.4 %collective-permute-start.20 = (bf16[2,2,2,112,512]{4,3,1,0,2:T(8,128)(2,1)S(1)}, bf16[2,2,2,112,512]{4,3,1,0,2:T(8,128)(2,1)S(1)}, u32[]{:S(2)}, u32[]{:S(2)}) collective-permute-start(bf16[2,2,2,112,512]{4,3,1,0,2:T(8,128)(2,1)S(1)} %bitcast.307), channel_id=1, source_target_pairs={{0,4},{1,5},{2,6},{3,7},{4,0},{5,1},{6,2},{7,3},{8,12},{9,13},{10,... | collective-permute-start | bytes 2752520 | tf_op jit(solution)/shard_map/ppermute | solution.py:1204
  345.1 21.8 %collective-permute-start.26 = (bf16[256,512]{1,0:T(8,128)(2,1)S(1)}, bf16[256,512]{1,0:T(8,128)(2,1)S(1)}, u32[]{:S(2)}, u32[]{:S(2)}) collective-permute-start(bf16[256,512]{1,0:T(8,128)(2,1)S(1)} %get-tuple-element.263), channel_id=1, source_target_pairs={{0,8},{1,9},{2,10},{3,11},{4,12},{5,13},{6,14},{7,15},{8,0},{9,1},... | collective-permute-start | bytes 786440 | tf_op jit(solution)/shard_map/ppermute | solution.py:1204
  345.2 26.0 %collective-permute-start.27 = (bf16[256,512]{1,0:T(8,128)(2,1)S(1)}, bf16[256,512]{1,0:T(8,128)(2,1)S(1)}, u32[]{:S(2)}, u32[]{:S(2)}) collective-permute-start(bf16[256,512]{1,0:T(8,128)(2,1)S(1)} %get-tuple-element.264), channel_id=1, source_target_pairs={{0,16},{1,17},{2,18},{3,19},{4,20},{5,21},{6,22},{7,23},{8,24},{9,... | collective-permute-start | bytes 786440 | tf_op jit(solution)/shard_map/ppermute | solution.py:1204
  352.7 18.4 %collective-permute-start.28 = (bf16[256,512]{1,0:T(8,128)(2,1)S(1)}, bf16[256,512]{1,0:T(8,128)(2,1)S(1)}, u32[]{:S(2)}, u32[]{:S(2)}) collective-permute-start(bf16[256,512]{1,0:T(8,128)(2,1)S(1)} %get-tuple-element.265), channel_id=1, source_target_pairs={{0,24},{1,25},{2,26},{3,27},{4,28},{5,29},{6,30},{7,31},{8,16},{9,... | collective-permute-start | bytes 786440 | tf_op jit(solution)/shard_map/ppermute | solution.py:1204
  360.5 12.4 %collective-permute-start.23 = (bf16[2,2,96,512]{3,2,1,0:T(8,128)(2,1)S(1)}, bf16[2,2,96,512]{3,2,1,0:T(8,128)(2,1)S(1)}, u32[]{:S(2)}, u32[]{:S(2)}) collective-permute-start(bf16[2,2,96,512]{3,2,1,0:T(8,128)(2,1)S(1)} %dynamic-slice_bitcast_fusion.3), channel_id=1, source_target_pairs={{0,4},{1,5},{2,6},{3,7},{4,0},{5,1},{6,2},{7,3},{8,12},{9,13},{10,... | collective-permute-start | bytes 1179656 | tf_op jit(solution)/shard_map/ppermute | solution.py:1204
  366.3 9.6 %collective-permute-start.21 = (bf16[2,2,112,512]{3,2,1,0:T(8,128)(2,1)S(1)}, bf16[2,2,112,512]{3,2,1,0:T(8,128)(2,1)S(1)}, u32[]{:S(2)}, u32[]{:S(2)}) collective-permute-start(bf16[2,2,112,512]{3,2,1,0:T(8,128)(2,1)S(1)} %dynamic-slice_bitcast_fusion.2), channel_id=1, source_target_pairs={{0,2},{1,3},{2,0},{3,1},{4,6},{5,7},{6,4},{7,5},{8,10},{9,11},{10,... | collective-permute-start | bytes 1376264 | tf_op jit(solution)/shard_map/ppermute | solution.py:1204
  376.9 14.9 %collective-permute-start.29 = (bf16[208,512]{1,0:T(8,128)(2,1)}, bf16[208,512]{1,0:T(8,128)(2,1)S(1)}, u32[]{:S(2)}, u32[]{:S(2)}) collective-permute-start(bf16[208,512]{1,0:T(8,128)(2,1)} %get-tuple-element.223), channel_id=1, source_target_pairs={{0,8},{1,9},{2,10},{3,11},{4,12},{5,13},{6,14},{7,15},{8,0},{9,1},... | collective-permute-start | bytes 638984 | tf_op jit(solution)/shard_map/ppermute | solution.py:1204
  377.4 22.2 %collective-permute-start.30 = (bf16[208,512]{1,0:T(8,128)(2,1)}, bf16[208,512]{1,0:T(8,128)(2,1)}, u32[]{:S(2)}, u32[]{:S(2)}) collective-permute-start(bf16[208,512]{1,0:T(8,128)(2,1)} %get-tuple-element.224), channel_id=1, source_target_pairs={{0,16},{1,17},{2,18},{3,19},{4,20},{5,21},{6,22},{7,23},{8,24},{9,... | collective-permute-start | bytes 638984 | tf_op jit(solution)/shard_map/ppermute | solution.py:1204
  385.1 14.5 %collective-permute-start.31 = (bf16[208,512]{1,0:T(8,128)(2,1)}, bf16[208,512]{1,0:T(8,128)(2,1)}, u32[]{:S(2)}, u32[]{:S(2)}) collective-permute-start(bf16[208,512]{1,0:T(8,128)(2,1)} %get-tuple-element.225), channel_id=1, source_target_pairs={{0,24},{1,25},{2,26},{3,27},{4,28},{5,29},{6,30},{7,31},{8,16},{9,... | collective-permute-start | bytes 638984 | tf_op jit(solution)/shard_map/ppermute | solution.py:1204
  400.8 1.7 copy-start.25
  400.8 1.7 copy-start.26
  400.8 1.7 copy-start.32
  (8 other events, 10.8 us)
